TPU v7x, 128 devices: a whole 4x4x4 slice. The times are simulated.
128 devices in a mesh: gx: 4 (over z), gy: 32 (over x, y, core).
Axes of the slice: x: 4, y: 4, z: 4, core: 2. Of those that a mesh axis runs over, the one named last changes fastest.
Arguments:
- fine_rhs: float32 [16384, 512], P(('gx', 'gy')), may hold values from -6 to 6
- fine_guess: float32 [16384, 512], P(('gx', 'gy')), may hold values from -3 to 3
- fine_coef: float32 [16384, 512], P(('gx', 'gy')), may hold values from 0.2 to 5
- fine_links: int32 [16384, 6], P(('gx', 'gy')), may hold values from -1 to 16383, as said below
- parent_owner: int32 [16384, 1], P(('gx', 'gy')), may hold values from 0 to 127, as said below
- coarse_coef: float32 [4096, 512], P(('gx', 'gy')), may hold values from 0.2 to 5
- coarse_links: int32 [4096, 6], P(('gx', 'gy')), may hold values from -1 to 4095, as said below
Outputs:
- fine_solution: float32 [16384, 512], P(('gx', 'gy'))
- coarse_correction: float32 [4096, 512], P(('gx', 'gy'))
Inputs may be any that keep to these rules, and one draw needn't show every extreme that they name: fine_links[b, 2k + 1] names the fine brick across brick b's upper face along dimension k and fine_links[b, 2k] the one across its lower face, -1 at the domain's boundary. The relation is symmetric: if fine_links[b, f] = c then fine_links[c, f xor 1] = b. The brick across an upper face lies on the same device or the next one in gx+gy order, the brick across a lower face on the same device or the previous one. `coarse_links`: as for fine_links, over the 4096 coarse brick slots with 32 slots a device. `parent_owner`: the parent of a fine brick on device d lies on device d - 1, d or d + 1 in gx+gy order; along a device's bricks the owners never fall. At most 64 fine bricks of one device have their parent on the previous device and at most 64 on the next; some device has exactly 64 on the next.
All inputs are finite; a program needn't handle non-finite values.
Results may differ from a plain program's by a relative error of at most 0.0003.
Values sent between devices are 32-bit elements; how exact they have to be, the bound alone decides.
A program may use at most 64 MiB of HBM per device.

v0:
```python
import jax
import jax.numpy as jnp
import numpy as np
from jax import lax
from jax.sharding import PartitionSpec as P

B = 8
SWEEPS = 3


THETA = 1.25
DELTA = 0.75
SIGMA = THETA / DELTA
OPPOSITE = np.array([1, 0, 3, 2, 5, 4], dtype=np.int32)


def from_behind(value, axis, by):
    devices = lax.axis_size(axis)
    pairs = [(i, i + by) for i in range(devices) if 0 <= i + by < devices]
    return lax.ppermute(value, axis, pairs)


def exact_dot(left, right):
    return jnp.dot(left, right, precision=lax.Precision.HIGHEST, preferred_element_type=jnp.float32)


def spread_table(row_ids, width):
    return (row_ids[:, None] == jnp.arange(width, dtype=jnp.int32)[None, :]).astype(jnp.float32)


def collect_table(row_ids, width):
    return (jnp.arange(width, dtype=jnp.int32)[:, None] == row_ids[None, :]).astype(jnp.float32)


def cells_last(flat_rows, edge_len):
    return flat_rows.T.reshape(edge_len, edge_len, edge_len, flat_rows.shape[0])


def cells_first(volume):
    return volume.reshape(-1, volume.shape[-1]).T


def face_stack(volume):
    edge_len = volume.shape[0]
    face_list = []
    for dimension in range(3):
        face_list.append(lax.index_in_dim(volume, 0, dimension, keepdims=False))
        face_list.append(lax.index_in_dim(volume, edge_len - 1, dimension, keepdims=False))
    return jnp.stack(face_list, axis=0)


def neighbor_values(volume, ghosts):
    edge_len = volume.shape[0]
    result = []
    for dimension in range(3):
        lower = jnp.expand_dims(ghosts[2 * dimension], dimension)
        upper = jnp.expand_dims(ghosts[2 * dimension + 1], dimension)
        result.append(
            jnp.concatenate(
                [lower, lax.slice_in_dim(volume, 0, edge_len - 1, axis=dimension)], axis=dimension
            )
        )
        result.append(
            jnp.concatenate(
                [lax.slice_in_dim(volume, 1, edge_len, axis=dimension), upper], axis=dimension
            )
        )
    return result


def face_weights(coef_volume, coef_ghosts):
    weights = [0.5 * (coef_volume + other) for other in neighbor_values(coef_volume, coef_ghosts)]
    diagonal = weights[0]
    for weight in weights[1:]:
        diagonal = diagonal + weight
    return (weights, diagonal)


def operate(volume, weights, ghost_fn):
    result = jnp.zeros_like(volume)
    for weight, other in zip(weights, neighbor_values(volume, ghost_fn(volume, False))):
        result = result + weight * (volume - other)
    return result


def smooth(start, source, weights, diagonal, ghost_fn, from_zero):
    solution = start
    rho_now = 1.0 / SIGMA
    update = None
    for sweep_at in range(SWEEPS):
        if sweep_at == 0 and from_zero:
            residual = source
        else:
            residual = source - operate(solution, weights, ghost_fn)
        scaled = residual / diagonal
        if sweep_at == 0:
            update = scaled / THETA
        else:
            rho_next = 1.0 / (2.0 * SIGMA - rho_now)
            update = rho_next * rho_now * update + 2.0 * rho_next / DELTA * scaled
            rho_now = rho_next
        solution = solution + update
    return solution


def restrict(residual):
    half = residual.shape[0] // 2
    count = residual.shape[-1]
    summed = residual.reshape(half, 2, half, 2, half, 2, count).sum(axis=(1, 3, 5)) * 0.5
    return summed.reshape(half * half * half, count)


def prolong(values, edge_len):
    count = values.shape[-1]
    half = edge_len // 2
    shaped = values.reshape(half, 1, half, 1, half, 1, count)
    shaped = jnp.broadcast_to(shaped, (half, 2, half, 2, half, 2, count))
    return shaped.reshape(edge_len, edge_len, edge_len, count)


def level_selector(link_ids, brick_count):
    my_index = lax.axis_index(("gx", "gy"))
    safe_ids = jnp.maximum(link_ids, 0)
    pool_row = (safe_ids // brick_count - my_index + 1) * brick_count + safe_ids % brick_count
    pool_row = jnp.clip(pool_row, 0, 3 * brick_count - 1)
    pool_row = jnp.where(link_ids >= 0, pool_row, -1)
    rows_all = jnp.arange(3 * brick_count, dtype=jnp.int32)
    return (rows_all[None, :, None] == pool_row.T[:, None, :]).astype(jnp.float32)


def device_ghosts(volume, selector, link_ids, keep_own, is_fine):
    edge_len = volume.shape[0]
    brick_count = volume.shape[-1]
    face_area = edge_len * edge_len
    face_set = face_stack(volume)
    flat_faces = face_set.reshape(6, face_area, brick_count)
    whole_faces = flat_faces.reshape(6 * face_area, brick_count)
    payloads = (whole_faces, whole_faces)
    if is_fine:
        received = [
            from_behind(payload, ("gx", "gy"), step_by)
            for payload, step_by in zip(payloads, (1, -1))
        ]
    else:
        received = [
            from_behind(payload, ("gx", "gy"), step_by)
            for payload, step_by in zip(payloads, (1, -1))
        ]
    earlier = received[0].reshape(6, face_area, brick_count)
    later_faces = received[1].reshape(6, face_area, brick_count)
    face_pool = jnp.concatenate([earlier, flat_faces, later_faces], axis=2)
    opposite_pool = face_pool[OPPOSITE]
    picked = jnp.einsum(
        "fcr,frb->fcb",
        opposite_pool,
        selector,
        precision=lax.Precision.HIGHEST,
        preferred_element_type=jnp.float32,
    )
    picked = picked.reshape(6, edge_len, edge_len, brick_count)
    if keep_own:
        is_live = (link_ids >= 0).T[:, None, None, :]
        return jnp.where(is_live, picked, face_set)
    return picked


def on_device(fine_rhs, fine_guess, fine_coef, fine_links, parent_owner, coarse_coef, coarse_links):
    fine_count = fine_rhs.shape[0]
    coarse_count = coarse_coef.shape[0]
    fine_selector = level_selector(fine_links, fine_count)
    coarse_selector = level_selector(coarse_links, coarse_count)

    def fine_ghosts(volume, keep_own):
        return device_ghosts(volume, fine_selector, fine_links, keep_own, True)

    def coarse_ghosts(volume, keep_own):
        return device_ghosts(volume, coarse_selector, coarse_links, keep_own, False)

    half = B // 2
    octant_cells = half * half * half
    slot_cap = fine_count // 2
    total_rows = 8 * coarse_count
    source = cells_last(fine_rhs, B)
    coef_volume = cells_last(fine_coef, B)
    weights, diagonal = face_weights(coef_volume, fine_ghosts(coef_volume, True))
    smoothed = smooth(cells_last(fine_guess, B), source, weights, diagonal, fine_ghosts, False)
    residual = source - operate(smoothed, weights, fine_ghosts)
    restricted = restrict(residual)
    my_index = lax.axis_index(("gx", "gy"))
    owner_dev = parent_owner[:, 0]
    go_prev = (owner_dev == my_index - 1).astype(jnp.int32)
    go_next = (owner_dev == my_index + 1).astype(jnp.int32)
    stay_here = (owner_dev == my_index).astype(jnp.int32)
    prev_rank = jnp.cumsum(go_prev, dtype=jnp.int32) - go_prev
    next_rank = jnp.cumsum(go_next, dtype=jnp.int32) - go_next
    stay_rank = jnp.cumsum(stay_here, dtype=jnp.int32) - stay_here
    prev_where = jnp.where(go_prev == 1, prev_rank, -1)
    next_where = jnp.where(go_next == 1, next_rank, -1)
    prev_table = spread_table(prev_where, slot_cap)
    next_table = spread_table(next_where, slot_cap)
    prev_buffer = exact_dot(restricted, prev_table)
    prev_marks = jnp.sum(prev_table, axis=0)
    next_buffer = exact_dot(restricted, next_table)
    next_marks = jnp.sum(next_table, axis=0)
    sent_pairs = (((next_buffer, next_marks), 1), ((prev_buffer, prev_marks), -1))
    arrived = [
        from_behind((payload[0], payload[1]), ("gx", "gy"), step_by)
        for payload, step_by in sent_pairs
    ]
    from_prev_values, from_prev_marks = arrived[0]
    from_next_values, from_next_marks = arrived[1]
    prev_total = jnp.sum(from_prev_marks).astype(jnp.int32)
    stay_total = jnp.sum(stay_here, dtype=jnp.int32)
    slot_ids = jnp.arange(slot_cap, dtype=jnp.int32)
    pos_from_prev = jnp.where(from_prev_marks > 0.5, slot_ids, total_rows)
    pos_stay = jnp.where(stay_here == 1, prev_total + stay_rank, total_rows)
    pos_from_next = jnp.where(from_next_marks > 0.5, prev_total + stay_total + slot_ids, total_rows)

    def column_of(position):
        return jnp.where(position < total_rows, position % 8 * coarse_count + position // 8, -1)

    col_prev = column_of(pos_from_prev)
    col_stay = column_of(pos_stay)
    col_next = column_of(pos_from_next)
    all_columns = jnp.concatenate([col_prev, col_stay, col_next], axis=0)
    all_values = jnp.concatenate([from_prev_values, restricted, from_next_values], axis=1)
    flat_source = exact_dot(all_values, spread_table(all_columns, total_rows))
    coarse_source = flat_source.reshape(half, half, half, 2, 2, 2, coarse_count)
    coarse_source = coarse_source.transpose(3, 0, 4, 1, 5, 2, 6).reshape(B, B, B, coarse_count)
    coarse_volume = cells_last(coarse_coef, B)
    coarse_weights, coarse_diagonal = face_weights(
        coarse_volume, coarse_ghosts(coarse_volume, True)
    )
    correction = smooth(
        jnp.zeros((B, B, B, coarse_count), jnp.float32),
        coarse_source,
        coarse_weights,
        coarse_diagonal,
        coarse_ghosts,
        True,
    )
    flat_correction = correction.reshape(2, half, 2, half, 2, half, coarse_count)
    flat_correction = flat_correction.transpose(1, 3, 5, 0, 2, 4, 6).reshape(
        octant_cells, total_rows
    )
    back_to_prev = exact_dot(flat_correction, collect_table(col_prev, total_rows))
    back_to_next = exact_dot(flat_correction, collect_table(col_next, total_rows))
    stay_values = exact_dot(flat_correction, collect_table(col_stay, total_rows))
    return_pairs = ((back_to_prev, -1), (back_to_next, 1))
    returned = [from_behind(payload, ("gx", "gy"), step_by) for payload, step_by in return_pairs]
    got_from_next = returned[0]
    got_from_prev = returned[1]
    prev_values = exact_dot(got_from_prev, collect_table(prev_where, slot_cap))
    next_values = exact_dot(got_from_next, collect_table(next_where, slot_cap))
    back_values = stay_values + prev_values + next_values
    corrected = smoothed + prolong(back_values, B)
    fine_solution = smooth(corrected, source, weights, diagonal, fine_ghosts, False)
    return (cells_first(fine_solution), cells_first(correction))


def solution(mesh):
    placed = (
        P(("gx", "gy"), None),
        P(("gx", "gy"), None),
        P(("gx", "gy"), None),
        P(("gx", "gy"), None),
        P(("gx", "gy"), None),
        P(("gx", "gy"), None),
        P(("gx", "gy"), None),
    )
    return jax.shard_map(
        on_device,
        mesh=mesh,
        in_specs=placed,
        out_specs=(P(("gx", "gy"), None), P(("gx", "gy"), None)),
        check_vma=False,
    )
```

profile of v0, /device:TPU:32, one launch (start us, length us, event | category | flops | bytes accessed | tf_op | source)
XLA Modules:
  0.0 312.9 jit_solution(12025571929171120035)
XLA Ops:
  1.9 2.1 collective-permute-start
  4.0 7.9 %collective-permute-start.1 = (f32[384,128]{1,0:T(8,128)S(1)}, f32[384,128]{1,0:T(8,128)S(1)}, u32[]{:S(2)}, u32[]{:S(2)}) collective-permute-start(f32[384,128]{1,0:T(8,128)S(1)} %bitcast.1377), channel_id=1, source_target_pairs={{1,0},{2,1},{3,2},{4,3},{5,4},{6,5},{7,6},{8,7},{9,8},{10,9},{11,1... | collective-permute-start | bytes 589832 | tf_op jit(solution)/shard_map/ppermute | solution.py:20
  12.1 1.9 collective-permute-start.14
  14.1 7.9 %collective-permute-start.15 = (f32[384,32]{1,0:T(8,128)S(1)}, f32[384,32]{1,0:T(8,128)}, u32[]{:S(2)}, u32[]{:S(2)}) collective-permute-start(f32[384,32]{1,0:T(8,128)S(1)} %bitcast.1379), channel_id=1, source_target_pairs={{1,0},{2,1},{3,2},{4,3},{5,4},{6,5},{7,6},{8,7},{9,8},{10,9},{11,1... | collective-permute-start | bytes 147464 | tf_op jit(solution)/shard_map/ppermute | solution.py:20
  22.4 1.9 collective-permute-start.12
  34.2 7.9 %collective-permute-start.13 = (f32[64]{0:T(128)S(1)}, f32[64]{0:T(128)S(1)}, u32[]{:S(2)}, u32[]{:S(2)}) collective-permute-start(f32[64]{0:T(128)S(1)} %convert_reduce_fusion), channel_id=1, source_target_pairs={{1,0},{2,1},{3,2},{4,3},{5,4},{6,5},{7,6},{8,7},{9,8},{10,9},{11,1... | collective-permute-start | bytes 776 | tf_op jit(solution)/shard_map/ppermute | solution.py:20
  44.1 1.9 collective-permute-start.2
  46.7 7.9 %collective-permute-start.3 = (f32[384,128]{1,0:T(8,128)}, f32[384,128]{1,0:T(8,128)}, u32[]{:S(2)}, u32[]{:S(2)}) collective-permute-start(f32[384,128]{1,0:T(8,128)} %bitcast.1426), channel_id=1, source_target_pairs={{1,0},{2,1},{3,2},{4,3},{5,4},{6,5},{7,6},{8,7},{9,8},{10,9},{11,1... | collective-permute-start | bytes 589832 | tf_op jit(solution)/shard_map/ppermute | solution.py:20
  62.6 2.9 multiply_add_fusion.2
  65.6 1.9 collective-permute-start.4
  67.6 7.9 %collective-permute-start.5 = (f32[384,128]{1,0:T(8,128)S(1)}, f32[384,128]{1,0:T(8,128)S(1)}, u32[]{:S(2)}, u32[]{:S(2)}) collective-permute-start(f32[384,128]{1,0:T(8,128)S(1)} %bitcast.1428), channel_id=1, source_target_pairs={{1,0},{2,1},{3,2},{4,3},{5,4},{6,5},{7,6},{8,7},{9,8},{10,9},{11,1... | collective-permute-start | bytes 589832 | tf_op jit(solution)/shard_map/ppermute | solution.py:20
  82.6 2.5 gather_fusion.2
  85.1 1.8 fusion.5
  87.0 2.3 fusion.209
  89.4 1.9 collective-permute-start.6
  91.3 7.9 %collective-permute-start.7 = (f32[384,128]{1,0:T(8,128)S(1)}, f32[384,128]{1,0:T(8,128)S(1)}, u32[]{:S(2)}, u32[]{:S(2)}) collective-permute-start(f32[384,128]{1,0:T(8,128)S(1)} %bitcast.1430), channel_id=1, source_target_pairs={{1,0},{2,1},{3,2},{4,3},{5,4},{6,5},{7,6},{8,7},{9,8},{10,9},{11,1... | collective-permute-start | bytes 589832 | tf_op jit(solution)/shard_map/ppermute | solution.py:20
  105.5 2.5 gather_fusion.3
  108.0 1.7 fusion.4
  114.3 1.9 collective-permute-start.8
  116.2 8.0 %collective-permute-start.9 = (f32[384,128]{1,0:T(8,128)S(1)}, f32[384,128]{1,0:T(8,128)S(1)}, u32[]{:S(2)}, u32[]{:S(2)}) collective-permute-start(f32[384,128]{1,0:T(8,128)S(1)} %bitcast.1432), channel_id=1, source_target_pairs={{1,0},{2,1},{3,2},{4,3},{5,4},{6,5},{7,6},{8,7},{9,8},{10,9},{11,1... | collective-permute-start | bytes 589832 | tf_op jit(solution)/shard_map/ppermute | solution.py:20
  128.1 2.5 gather_fusion.4
  130.6 1.8 fusion.3
  138.0 5.8 %subtract_reduce_fusion = f32[4,4,4,128]{3,2,1,0:T(4,128)S(1)} fusion(f32[4,2,4,2,4,2,128]{6,5,4,3,2,1,0:T(2,128)S(1)} %bitcast.1251, f32[4,2,4,2,4,2,128]{6,5,4,3,2,1,0:T(2,128)S(1)} %bitcast.1319, f32[4,2,4,2,4,2,128]{6,5,4,3,2,1,0:T(2,128)S(1)} %bitcast.1318, f32[4,2,4,2,4,2,128]{6,5,4,3,2,1,0:T(2,128)S(1)} %bitcast.1317, ...), kind=kLoop, calls=%fused_computation.451 | loop fusion | flops 6742016 | bytes 8683520 | tf_op jit(solution)/shard_map/reduce_sum | solution.py:109
  144.2 1.9 collective-permute-start.10
  146.2 8.0 %collective-permute-start.11 = (f32[64,64]{1,0:T(8,128)S(1)}, f32[64,64]{1,0:T(8,128)S(1)}, u32[]{:S(2)}, u32[]{:S(2)}) collective-permute-start(f32[64,64]{1,0:T(8,128)S(1)} %fusion.174), channel_id=1, source_target_pairs={{1,0},{2,1},{3,2},{4,3},{5,4},{6,5},{7,6},{8,7},{9,8},{10,9},{11,1... | collective-permute-start | bytes 49160 | tf_op jit(solution)/shard_map/ppermute | solution.py:20
  157.4 2.5 fusion.156
  160.0 1.9 collective-permute-start.16
  161.9 7.9 %collective-permute-start.17 = (f32[384,32]{1,0:T(8,128)S(1)}, f32[384,32]{1,0:T(8,128)S(1)}, u32[]{:S(2)}, u32[]{:S(2)}) collective-permute-start(f32[384,32]{1,0:T(8,128)S(1)} %bitcast.1434), channel_id=1, source_target_pairs={{1,0},{2,1},{3,2},{4,3},{5,4},{6,5},{7,6},{8,7},{9,8},{10,9},{11,1... | collective-permute-start | bytes 147464 | tf_op jit(solution)/shard_map/ppermute | solution.py:20
  173.8 2.1 gather_fusion.6
  175.9 1.2 fusion.162
  177.8 1.4 copy.577
  179.2 1.4 copy.578
  180.6 1.4 copy.579
  182.0 1.4 copy.581
  183.5 1.4 copy.583
  184.9 1.4 copy.585
  186.3 1.7 pad_maximum_fusion.44
  188.0 1.5 pad_maximum_fusion.45
  189.6 1.6 pad_maximum_fusion.46
  191.2 1.5 pad_maximum_fusion.47
  192.7 2.5 add_add_fusion.1
  195.4 1.9 collective-permute-start.18
  197.3 8.0 %collective-permute-start.19 = (f32[384,32]{1,0:T(8,128)S(1)}, f32[384,32]{1,0:T(8,128)S(1)}, u32[]{:S(2)}, u32[]{:S(2)}) collective-permute-start(f32[384,32]{1,0:T(8,128)S(1)} %bitcast.1436), channel_id=1, source_target_pairs={{1,0},{2,1},{3,2},{4,3},{5,4},{6,5},{7,6},{8,7},{9,8},{10,9},{11,1... | collective-permute-start | bytes 147464 | tf_op jit(solution)/shard_map/ppermute | solution.py:20
  209.4 2.2 gather_fusion.7
  218.6 1.3 pad_maximum_fusion.54
  221.1 2.3 add_bitcast_fusion
  225.9 3.6 %fusion.25 = f32[512,32]{1,0:T(8,128)} fusion(f32[512,32]{1,0:T(8,128)S(1)} %bitcast.1256, f32[8,8,8,32]{3,2,1,0:T(8,128)} %copy-done.57, f32[8,8,8,32]{3,2,1,0:T(8,128)} %copy-done.56, f32[8,8,8,32]{3,2,1,0:T(8,128)} %copy-done.55, f32[8,8,8,32]{3,2,1,0:T(8,128)} %copy-done.54, f32[8,8,8,32]{3,2,1,0:T(8,128)} %copy-done.53, f32[8,8,8,32]{3,2,1,0:T(8,128)} %copy-done.52, ...), kind=kLoop, calls=%fused_computation.247 | loop fusion | flops 1064960 | bytes 1376256 | tf_op jit(solution)/shard_map/add | solution.py:102
  229.5 1.9 collective-permute-start.20
  231.6 1.7 copy.623
  233.3 8.0 %collective-permute-start.21 = (f32[64,64]{1,0:T(8,128)S(1)}, f32[64,64]{1,0:T(8,128)S(1)}, u32[]{:S(2)}, u32[]{:S(2)}) collective-permute-start(f32[64,64]{1,0:T(8,128)S(1)} %fusion.160), channel_id=1, source_target_pairs={{1,0},{2,1},{3,2},{4,3},{5,4},{6,5},{7,6},{8,7},{9,8},{10,9},{11,1... | collective-permute-start | bytes 49160 | tf_op jit(solution)/shard_map/ppermute | solution.py:20
  243.3 1.9 collective-permute-start.22
  245.3 8.1 %collective-permute-start.23 = (f32[384,128]{1,0:T(8,128)S(1)}, f32[384,128]{1,0:T(8,128)S(1)}, u32[]{:S(2)}, u32[]{:S(2)}) collective-permute-start(f32[384,128]{1,0:T(8,128)S(1)} %bitcast.1438), channel_id=1, source_target_pairs={{1,0},{2,1},{3,2},{4,3},{5,4},{6,5},{7,6},{8,7},{9,8},{10,9},{11,1... | collective-permute-start | bytes 589832 | tf_op jit(solution)/shard_map/ppermute | solution.py:20
  257.2 2.5 gather_fusion.8
  259.6 1.7 fusion.2
  265.6 1.9 collective-permute-start.24
  267.5 8.0 %collective-permute-start.25 = (f32[384,128]{1,0:T(8,128)S(1)}, f32[384,128]{1,0:T(8,128)S(1)}, u32[]{:S(2)}, u32[]{:S(2)}) collective-permute-start(f32[384,128]{1,0:T(8,128)S(1)} %bitcast.1440), channel_id=1, source_target_pairs={{1,0},{2,1},{3,2},{4,3},{5,4},{6,5},{7,6},{8,7},{9,8},{10,9},{11,1... | collective-permute-start | bytes 589832 | tf_op jit(solution)/shard_map/ppermute | solution.py:20
  277.3 1.4 collective-permute-done.25
  279.6 2.5 gather_fusion.9
  282.1 1.7 fusion.1
  288.1 1.9 collective-permute-start.26
  290.0 8.0 %collective-permute-start.27 = (f32[384,128]{1,0:T(8,128)S(1)}, f32[384,128]{1,0:T(8,128)S(1)}, u32[]{:S(2)}, u32[]{:S(2)}) collective-permute-start(f32[384,128]{1,0:T(8,128)S(1)} %bitcast.1442), channel_id=1, source_target_pairs={{1,0},{2,1},{3,2},{4,3},{5,4},{6,5},{7,6},{8,7},{9,8},{10,9},{11,1... | collective-permute-start | bytes 589832 | tf_op jit(solution)/shard_map/ppermute | solution.py:20
  299.9 1.4 collective-permute-done.27
  306.2 4.9 %fusion.62 = f32[512,128]{1,0:T(8,128)} fusion(f32[8,8,8,128]{3,2,1,0:T(8,128)S(1)} %pad_maximum_fusion.73, f32[8,8,8,128]{3,2,1,0:T(8,128)S(1)} %pad_maximum_fusion.72, f32[8,8,8,128]{3,2,1,0:T(8,128)S(1)} %pad_maximum_fusion.71, f32[8,8,8,128]{3,2,1,0:T(8,128)S(1)} %pad_maximum_fusion.70, f32[8,8,8,128]{3,2,1,0:T(8,128)S(1)} %pad_maximum_fusion.69, ...), kind=kLoop, calls=%fused_computation.302 | loop fusion | flops 9961472 | bytes 12320768 | tf_op jit(solution)/shard_map/add | solution.py:102
  311.1 1.8 copy.622
  (565 shorter events, 93.9 us)
Async XLA Ops:
  0.6 11.2 %copy-start.104 = (f32[32,512]{1,0:T(8,128)S(1)}, f32[32,512]{1,0:T(8,128)}, u32[]{:S(2)}) copy-start(f32[32,512]{1,0:T(8,128)} %param.24) | copy-start | bytes 196612
  1.8 20.1 %copy-start.118 = (s32[128,1]{0,1:T(1,128)S(1)}, s32[128,1]{0,1:T(1,128)}, u32[]{:S(2)}) copy-start(s32[128,1]{0,1:T(1,128)} %param.23) | copy-start | bytes 1540
  1.9 22.5 %copy-start.99 = (f32[6,8,8,128]{3,2,1,0:T(8,128)}, f32[6,8,8,128]{3,2,1,0:T(8,128)S(1)}, u32[]{:S(2)}) copy-start(f32[6,8,8,128]{3,2,1,0:T(8,128)S(1)} %constant_dynamic-update-slice_fusion) | copy-start | bytes 589828
  1.9 22.5 %copy-start.105 = (s32[128,6]{0,1:T(8,128)S(1)}, s32[128,6]{0,1:T(8,128)}, u32[]{:S(2)}) copy-start(s32[128,6]{0,1:T(8,128)} %param.22) | copy-start | bytes 9220
  1.9 23.1 %copy-start.101 = (f32[128,512]{1,0:T(8,128)S(1)}, f32[128,512]{1,0:T(8,128)}, u32[]{:S(2)}) copy-start(f32[128,512]{1,0:T(8,128)} %param.20) | copy-start | bytes 786436
  1.9 55.4 %collective-permute-start = (f32[384,128]{1,0:T(8,128)S(1)}, f32[384,128]{1,0:T(8,128)S(1)}, u32[]{:S(2)}, u32[]{:S(2)}) collective-permute-start(f32[384,128]{1,0:T(8,128)S(1)} %bitcast.1376), channel_id=1, source_target_pairs={{0,1},{1,2},{2,3},{3,4},{4,5},{5,6},{6,7},{7,8},{8,9},{9,10},{10,1... | collective-permute-start | bytes 589832 | tf_op jit(solution)/shard_map/ppermute | solution.py:20
  4.0 53.3 %collective-permute-start.1 = (f32[384,128]{1,0:T(8,128)S(1)}, f32[384,128]{1,0:T(8,128)S(1)}, u32[]{:S(2)}, u32[]{:S(2)}) collective-permute-start(f32[384,128]{1,0:T(8,128)S(1)} %bitcast.1377), channel_id=1, source_target_pairs={{1,0},{2,1},{3,2},{4,3},{5,4},{6,5},{7,6},{8,7},{9,8},{10,9},{11,1... | collective-permute-start | bytes 589832 | tf_op jit(solution)/shard_map/ppermute | solution.py:20
  12.1 34.6 %collective-permute-start.14 = (f32[384,32]{1,0:T(8,128)S(1)}, f32[384,32]{1,0:T(8,128)}, u32[]{:S(2)}, u32[]{:S(2)}) collective-permute-start(f32[384,32]{1,0:T(8,128)S(1)} %bitcast.1378), channel_id=1, source_target_pairs={{0,1},{1,2},{2,3},{3,4},{4,5},{5,6},{6,7},{7,8},{8,9},{9,10},{10,1... | collective-permute-start | bytes 147464 | tf_op jit(solution)/shard_map/ppermute | solution.py:20
  14.1 40.5 %collective-permute-start.15 = (f32[384,32]{1,0:T(8,128)S(1)}, f32[384,32]{1,0:T(8,128)}, u32[]{:S(2)}, u32[]{:S(2)}) collective-permute-start(f32[384,32]{1,0:T(8,128)S(1)} %bitcast.1379), channel_id=1, source_target_pairs={{1,0},{2,1},{3,2},{4,3},{5,4},{6,5},{7,6},{8,7},{9,8},{10,9},{11,1... | collective-permute-start | bytes 147464 | tf_op jit(solution)/shard_map/ppermute | solution.py:20
  22.4 11.8 %collective-permute-start.12 = (f32[64]{0:T(128)S(1)}, f32[64]{0:T(128)S(1)}, u32[]{:S(2)}, u32[]{:S(2)}) collective-permute-start(f32[64]{0:T(128)S(1)} %convert_reduce_fusion.1), channel_id=1, source_target_pairs={{0,1},{1,2},{2,3},{3,4},{4,5},{5,6},{6,7},{7,8},{8,9},{9,10},{10,1... | collective-permute-start | bytes 776 | tf_op jit(solution)/shard_map/ppermute | solution.py:20
  30.8 123.4 %copy-start.4 = (f32[8,7,8,32]{3,2,1,0:T(8,128)}, f32[8,7,8,32]{3,2,1,0:T(8,128)S(1)}, u32[]{:S(2)}) copy-start(f32[8,7,8,32]{3,2,1,0:T(8,128)S(1)} %get-tuple-element.90) | copy-start | bytes 172036
  34.2 9.9 %collective-permute-start.13 = (f32[64]{0:T(128)S(1)}, f32[64]{0:T(128)S(1)}, u32[]{:S(2)}, u32[]{:S(2)}) collective-permute-start(f32[64]{0:T(128)S(1)} %convert_reduce_fusion), channel_id=1, source_target_pairs={{1,0},{2,1},{3,2},{4,3},{5,4},{6,5},{7,6},{8,7},{9,8},{10,9},{11,1... | collective-permute-start | bytes 776 | tf_op jit(solution)/shard_map/ppermute | solution.py:20
  43.5 12.9 %copy-start.114 = (s32[64]{0:T(128)}, s32[64]{0:T(128)S(1)}, u32[]{:S(2)}) copy-start(s32[64]{0:T(128)S(1)} %compare_select_fusion.4) | copy-start | bytes 772
  44.1 15.4 %collective-permute-start.2 = (f32[384,128]{1,0:T(8,128)}, f32[384,128]{1,0:T(8,128)}, u32[]{:S(2)}, u32[]{:S(2)}) collective-permute-start(f32[384,128]{1,0:T(8,128)} %bitcast.1425), channel_id=1, source_target_pairs={{0,1},{1,2},{2,3},{3,4},{4,5},{5,6},{6,7},{7,8},{8,9},{9,10},{10,1... | collective-permute-start | bytes 589832 | tf_op jit(solution)/shard_map/ppermute | solution.py:20
  46.1 10.3 %copy-start.116 = (s32[64]{0:T(128)}, s32[64]{0:T(128)S(1)}, u32[]{:S(2)}) copy-start(s32[64]{0:T(128)S(1)} %compare_select_fusion) | copy-start | bytes 772
  46.7 12.9 %collective-permute-start.3 = (f32[384,128]{1,0:T(8,128)}, f32[384,128]{1,0:T(8,128)}, u32[]{:S(2)}, u32[]{:S(2)}) collective-permute-start(f32[384,128]{1,0:T(8,128)} %bitcast.1426), channel_id=1, source_target_pairs={{1,0},{2,1},{3,2},{4,3},{5,4},{6,5},{7,6},{8,7},{9,8},{10,9},{11,1... | collective-permute-start | bytes 589832 | tf_op jit(solution)/shard_map/ppermute | solution.py:20
  65.6 16.1 %collective-permute-start.4 = (f32[384,128]{1,0:T(8,128)S(1)}, f32[384,128]{1,0:T(8,128)S(1)}, u32[]{:S(2)}, u32[]{:S(2)}) collective-permute-start(f32[384,128]{1,0:T(8,128)S(1)} %bitcast.1427), channel_id=1, source_target_pairs={{0,1},{1,2},{2,3},{3,4},{4,5},{5,6},{6,7},{7,8},{8,9},{9,10},{10,1... | collective-permute-start | bytes 589832 | tf_op jit(solution)/shard_map/ppermute | solution.py:20
  67.6 14.2 %collective-permute-start.5 = (f32[384,128]{1,0:T(8,128)S(1)}, f32[384,128]{1,0:T(8,128)S(1)}, u32[]{:S(2)}, u32[]{:S(2)}) collective-permute-start(f32[384,128]{1,0:T(8,128)S(1)} %bitcast.1428), channel_id=1, source_target_pairs={{1,0},{2,1},{3,2},{4,3},{5,4},{6,5},{7,6},{8,7},{9,8},{10,9},{11,1... | collective-permute-start | bytes 589832 | tf_op jit(solution)/shard_map/ppermute | solution.py:20
  89.4 15.2 %collective-permute-start.6 = (f32[384,128]{1,0:T(8,128)S(1)}, f32[384,128]{1,0:T(8,128)S(1)}, u32[]{:S(2)}, u32[]{:S(2)}) collective-permute-start(f32[384,128]{1,0:T(8,128)S(1)} %bitcast.1429), channel_id=1, source_target_pairs={{0,1},{1,2},{2,3},{3,4},{4,5},{5,6},{6,7},{7,8},{8,9},{9,10},{10,1... | collective-permute-start | bytes 589832 | tf_op jit(solution)/shard_map/ppermute | solution.py:20
  91.3 13.3 %collective-permute-start.7 = (f32[384,128]{1,0:T(8,128)S(1)}, f32[384,128]{1,0:T(8,128)S(1)}, u32[]{:S(2)}, u32[]{:S(2)}) collective-permute-start(f32[384,128]{1,0:T(8,128)S(1)} %bitcast.1430), channel_id=1, source_target_pairs={{1,0},{2,1},{3,2},{4,3},{5,4},{6,5},{7,6},{8,7},{9,8},{10,9},{11,1... | collective-permute-start | bytes 589832 | tf_op jit(solution)/shard_map/ppermute | solution.py:20
  100.0 9.7 %copy-start.76 = (f32[7,8,8,128]{3,2,1,0:T(8,128)}, f32[7,8,8,128]{3,2,1,0:T(8,128)S(1)}, u32[]{:S(2)}) copy-start(f32[7,8,8,128]{3,2,1,0:T(8,128)S(1)} %get-tuple-element.104) | copy-start | bytes 688132
  114.3 12.4 %collective-permute-start.8 = (f32[384,128]{1,0:T(8,128)S(1)}, f32[384,128]{1,0:T(8,128)S(1)}, u32[]{:S(2)}, u32[]{:S(2)}) collective-permute-start(f32[384,128]{1,0:T(8,128)S(1)} %bitcast.1431), channel_id=1, source_target_pairs={{0,1},{1,2},{2,3},{3,4},{4,5},{5,6},{6,7},{7,8},{8,9},{9,10},{10,1... | collective-permute-start | bytes 589832 | tf_op jit(solution)/shard_map/ppermute | solution.py:20
  116.2 11.0 %collective-permute-start.9 = (f32[384,128]{1,0:T(8,128)S(1)}, f32[384,128]{1,0:T(8,128)S(1)}, u32[]{:S(2)}, u32[]{:S(2)}) collective-permute-start(f32[384,128]{1,0:T(8,128)S(1)} %bitcast.1432), channel_id=1, source_target_pairs={{1,0},{2,1},{3,2},{4,3},{5,4},{6,5},{7,6},{8,7},{9,8},{10,9},{11,1... | collective-permute-start | bytes 589832 | tf_op jit(solution)/shard_map/ppermute | solution.py:20
  130.6 7.2 %copy-start.37 = (f32[8,8,8,128]{3,2,1,0:T(8,128)S(1)}, f32[8,8,8,128]{3,2,1,0:T(8,128)}, u32[]{:S(2)}) copy-start(f32[8,8,8,128]{3,2,1,0:T(8,128)} %pad_maximum_fusion.28) | copy-start | bytes 786436
  130.6 7.2 %copy-start.39 = (f32[8,8,8,128]{3,2,1,0:T(8,128)S(1)}, f32[8,8,8,128]{3,2,1,0:T(8,128)}, u32[]{:S(2)}) copy-start(f32[8,8,8,128]{3,2,1,0:T(8,128)} %pad_maximum_fusion.29) | copy-start | bytes 786436
  130.6 7.2 %copy-start.41 = (f32[8,8,8,128]{3,2,1,0:T(8,128)S(1)}, f32[8,8,8,128]{3,2,1,0:T(8,128)}, u32[]{:S(2)}) copy-start(f32[8,8,8,128]{3,2,1,0:T(8,128)} %get-tuple-element.208) | copy-start | bytes 786436
  132.4 5.5 %copy-start.33 = (f32[8,8,8,128]{3,2,1,0:T(8,128)S(1)}, f32[8,8,8,128]{3,2,1,0:T(8,128)}, u32[]{:S(2)}) copy-start(f32[8,8,8,128]{3,2,1,0:T(8,128)} %pad_maximum_fusion.26) | copy-start | bytes 786436
  132.4 5.5 %copy-start.35 = (f32[8,8,8,128]{3,2,1,0:T(8,128)S(1)}, f32[8,8,8,128]{3,2,1,0:T(8,128)}, u32[]{:S(2)}) copy-start(f32[8,8,8,128]{3,2,1,0:T(8,128)} %pad_maximum_fusion.27) | copy-start | bytes 786436
  132.4 5.4 %copy-start.29 = (f32[8,8,8,128]{3,2,1,0:T(8,128)S(1)}, f32[8,8,8,128]{3,2,1,0:T(8,128)}, u32[]{:S(2)}) copy-start(f32[8,8,8,128]{3,2,1,0:T(8,128)} %pad_maximum_fusion.22) | copy-start | bytes 786436
  132.4 5.4 %copy-start.31 = (f32[8,8,8,128]{3,2,1,0:T(8,128)S(1)}, f32[8,8,8,128]{3,2,1,0:T(8,128)}, u32[]{:S(2)}) copy-start(f32[8,8,8,128]{3,2,1,0:T(8,128)} %pad_maximum_fusion.23) | copy-start | bytes 786436
  133.5 4.4 %copy-start.25 = (f32[8,8,8,128]{3,2,1,0:T(8,128)S(1)}, f32[8,8,8,128]{3,2,1,0:T(8,128)}, u32[]{:S(2)}) copy-start(f32[8,8,8,128]{3,2,1,0:T(8,128)} %pad_maximum_fusion.20) | copy-start | bytes 786436
  133.5 4.4 %copy-start.27 = (f32[8,8,8,128]{3,2,1,0:T(8,128)S(1)}, f32[8,8,8,128]{3,2,1,0:T(8,128)}, u32[]{:S(2)}) copy-start(f32[8,8,8,128]{3,2,1,0:T(8,128)} %pad_maximum_fusion.21) | copy-start | bytes 786436
  138.0 5.9 %copy-start.110 = (s32[128]{0:T(128)S(1)}, s32[128]{0:T(128)}, u32[]{:S(2)}) copy-start(s32[128]{0:T(128)} %copy-done.109) | copy-start | bytes 1540
  138.0 6.1 %copy-start.113 = (s32[128]{0:T(128)S(1)}, s32[128]{0:T(128)}, u32[]{:S(2)}) copy-start(s32[128]{0:T(128)} %copy-done.112) | copy-start | bytes 1540
  138.0 16.2 %copy-start.7 = (f32[8,7,8,32]{3,2,1,0:T(8,128)S(1)}, f32[8,7,8,32]{3,2,1,0:T(8,128)}, u32[]{:S(2)}) copy-start(f32[8,7,8,32]{3,2,1,0:T(8,128)} %get-tuple-element.91) | copy-start | bytes 172036
  143.9 11.9 %copy-start.119 = (s32[256]{0:T(256)S(1)}, s32[256]{0:T(256)}, u32[]{:S(2)}) copy-start(s32[256]{0:T(256)} %pad_add_fusion) | copy-start | bytes 3076
  144.2 10.9 %collective-permute-start.10 = (f32[64,64]{1,0:T(8,128)S(1)}, f32[64,64]{1,0:T(8,128)S(1)}, u32[]{:S(2)}, u32[]{:S(2)}) collective-permute-start(f32[64,64]{1,0:T(8,128)S(1)} %fusion.175), channel_id=1, source_target_pairs={{0,1},{1,2},{2,3},{3,4},{4,5},{5,6},{6,7},{7,8},{8,9},{9,10},{10,1... | collective-permute-start | bytes 49160 | tf_op jit(solution)/shard_map/ppermute | solution.py:20
  146.2 9.6 %collective-permute-start.11 = (f32[64,64]{1,0:T(8,128)S(1)}, f32[64,64]{1,0:T(8,128)S(1)}, u32[]{:S(2)}, u32[]{:S(2)}) collective-permute-start(f32[64,64]{1,0:T(8,128)S(1)} %fusion.174), channel_id=1, source_target_pairs={{1,0},{2,1},{3,2},{4,3},{5,4},{6,5},{7,6},{8,7},{9,8},{10,9},{11,1... | collective-permute-start | bytes 49160 | tf_op jit(solution)/shard_map/ppermute | solution.py:20
  159.8 32.8 %copy-start.2 = (f32[8,8,8,32]{3,2,1,0:T(8,128)}, f32[8,8,8,32]{3,2,1,0:T(8,128)S(1)}, u32[]{:S(2)}) copy-start(f32[8,8,8,32]{3,2,1,0:T(8,128)S(1)} %get-tuple-element.22) | copy-start | bytes 196612
  160.0 12.4 %collective-permute-start.16 = (f32[384,32]{1,0:T(8,128)S(1)}, f32[384,32]{1,0:T(8,128)S(1)}, u32[]{:S(2)}, u32[]{:S(2)}) collective-permute-start(f32[384,32]{1,0:T(8,128)S(1)} %bitcast.1433), channel_id=1, source_target_pairs={{0,1},{1,2},{2,3},{3,4},{4,5},{5,6},{6,7},{7,8},{8,9},{9,10},{10,1... | collective-permute-start | bytes 147464 | tf_op jit(solution)/shard_map/ppermute | solution.py:20
  161.9 11.0 %collective-permute-start.17 = (f32[384,32]{1,0:T(8,128)S(1)}, f32[384,32]{1,0:T(8,128)S(1)}, u32[]{:S(2)}, u32[]{:S(2)}) collective-permute-start(f32[384,32]{1,0:T(8,128)S(1)} %bitcast.1434), channel_id=1, source_target_pairs={{1,0},{2,1},{3,2},{4,3},{5,4},{6,5},{7,6},{8,7},{9,8},{10,9},{11,1... | collective-permute-start | bytes 147464 | tf_op jit(solution)/shard_map/ppermute | solution.py:20
  186.3 6.4 %copy-start.86 = (f32[448,32]{1,0:T(8,128)S(1)}, f32[448,32]{1,0:T(8,128)}, u32[]{:S(2)}) copy-start(f32[448,32]{1,0:T(8,128)} %get-tuple-element.89) | copy-start | bytes 172036
  188.0 4.6 %copy-start.85 = (f32[448,32]{1,0:T(8,128)S(1)}, f32[448,32]{1,0:T(8,128)}, u32[]{:S(2)}) copy-start(f32[448,32]{1,0:T(8,128)} %get-tuple-element.88) | copy-start | bytes 172036
  195.4 12.5 %collective-permute-start.18 = (f32[384,32]{1,0:T(8,128)S(1)}, f32[384,32]{1,0:T(8,128)S(1)}, u32[]{:S(2)}, u32[]{:S(2)}) collective-permute-start(f32[384,32]{1,0:T(8,128)S(1)} %bitcast.1435), channel_id=1, source_target_pairs={{0,1},{1,2},{2,3},{3,4},{4,5},{5,6},{6,7},{7,8},{8,9},{9,10},{10,1... | collective-permute-start | bytes 147464 | tf_op jit(solution)/shard_map/ppermute | solution.py:20
  197.3 11.2 %collective-permute-start.19 = (f32[384,32]{1,0:T(8,128)S(1)}, f32[384,32]{1,0:T(8,128)S(1)}, u32[]{:S(2)}, u32[]{:S(2)}) collective-permute-start(f32[384,32]{1,0:T(8,128)S(1)} %bitcast.1436), channel_id=1, source_target_pairs={{1,0},{2,1},{3,2},{4,3},{5,4},{6,5},{7,6},{8,7},{9,8},{10,9},{11,1... | collective-permute-start | bytes 147464 | tf_op jit(solution)/shard_map/ppermute | solution.py:20
  215.2 5.8 %copy-start.59 = (f32[8,8,8,32]{3,2,1,0:T(8,128)S(1)}, f32[8,8,8,32]{3,2,1,0:T(8,128)}, u32[]{:S(2)}) copy-start(f32[8,8,8,32]{3,2,1,0:T(8,128)} %get-tuple-element.213) | copy-start | bytes 196612
  215.2 5.8 %copy-start.60 = (f32[8,8,8,32]{3,2,1,0:T(8,128)S(1)}, f32[8,8,8,32]{3,2,1,0:T(8,128)}, u32[]{:S(2)}) copy-start(f32[8,8,8,32]{3,2,1,0:T(8,128)} %get-tuple-element.68) | copy-start | bytes 196612
  216.3 4.7 %copy-start.52 = (f32[8,8,8,32]{3,2,1,0:T(8,128)}, f32[8,8,8,32]{3,2,1,0:T(8,128)S(1)}, u32[]{:S(2)}) copy-start(f32[8,8,8,32]{3,2,1,0:T(8,128)S(1)} %pad_maximum_fusion.50) | copy-start | bytes 196612
  216.3 4.7 %copy-start.51 = (f32[8,8,8,32]{3,2,1,0:T(8,128)S(1)}, f32[8,8,8,32]{3,2,1,0:T(8,128)}, u32[]{:S(2)}) copy-start(f32[8,8,8,32]{3,2,1,0:T(8,128)} %pad_maximum_fusion.47) | copy-start | bytes 196612
  216.3 4.7 %copy-start.58 = (f32[8,8,8,32]{3,2,1,0:T(8,128)S(1)}, f32[8,8,8,32]{3,2,1,0:T(8,128)}, u32[]{:S(2)}) copy-start(f32[8,8,8,32]{3,2,1,0:T(8,128)} %get-tuple-element.212) | copy-start | bytes 196612
  218.5 4.9 %copy-start.55 = (f32[8,8,8,32]{3,2,1,0:T(8,128)}, f32[8,8,8,32]{3,2,1,0:T(8,128)S(1)}, u32[]{:S(2)}) copy-start(f32[8,8,8,32]{3,2,1,0:T(8,128)S(1)} %pad_maximum_fusion.53) | copy-start | bytes 196612
  225.9 17.0 %copy-start.111 = (s32[128]{0:T(128)S(1)}, s32[128]{0:T(128)}, u32[]{:S(2)}) copy-start(s32[128]{0:T(128)} %copy-done.109) | copy-start | bytes 1540
  229.5 11.8 %collective-permute-start.20 = (f32[64,64]{1,0:T(8,128)S(1)}, f32[64,64]{1,0:T(8,128)S(1)}, u32[]{:S(2)}, u32[]{:S(2)}) collective-permute-start(f32[64,64]{1,0:T(8,128)S(1)} %fusion.159), channel_id=1, source_target_pairs={{0,1},{1,2},{2,3},{3,4},{4,5},{5,6},{6,7},{7,8},{8,9},{9,10},{10,1... | collective-permute-start | bytes 49160 | tf_op jit(solution)/shard_map/ppermute | solution.py:20
  233.3 9.6 %collective-permute-start.21 = (f32[64,64]{1,0:T(8,128)S(1)}, f32[64,64]{1,0:T(8,128)S(1)}, u32[]{:S(2)}, u32[]{:S(2)}) collective-permute-start(f32[64,64]{1,0:T(8,128)S(1)} %fusion.160), channel_id=1, source_target_pairs={{1,0},{2,1},{3,2},{4,3},{5,4},{6,5},{7,6},{8,7},{9,8},{10,9},{11,1... | collective-permute-start | bytes 49160 | tf_op jit(solution)/shard_map/ppermute | solution.py:20
  243.3 11.8 %collective-permute-start.22 = (f32[384,128]{1,0:T(8,128)S(1)}, f32[384,128]{1,0:T(8,128)S(1)}, u32[]{:S(2)}, u32[]{:S(2)}) collective-permute-start(f32[384,128]{1,0:T(8,128)S(1)} %bitcast.1437), channel_id=1, source_target_pairs={{0,1},{1,2},{2,3},{3,4},{4,5},{5,6},{6,7},{7,8},{8,9},{9,10},{10,1... | collective-permute-start | bytes 589832 | tf_op jit(solution)/shard_map/ppermute | solution.py:20
  245.3 11.0 %collective-permute-start.23 = (f32[384,128]{1,0:T(8,128)S(1)}, f32[384,128]{1,0:T(8,128)S(1)}, u32[]{:S(2)}, u32[]{:S(2)}) collective-permute-start(f32[384,128]{1,0:T(8,128)S(1)} %bitcast.1438), channel_id=1, source_target_pairs={{1,0},{2,1},{3,2},{4,3},{5,4},{6,5},{7,6},{8,7},{9,8},{10,9},{11,1... | collective-permute-start | bytes 589832 | tf_op jit(solution)/shard_map/ppermute | solution.py:20
  265.6 11.7 %collective-permute-start.24 = (f32[384,128]{1,0:T(8,128)S(1)}, f32[384,128]{1,0:T(8,128)S(1)}, u32[]{:S(2)}, u32[]{:S(2)}) collective-permute-start(f32[384,128]{1,0:T(8,128)S(1)} %bitcast.1439), channel_id=1, source_target_pairs={{0,1},{1,2},{2,3},{3,4},{4,5},{5,6},{6,7},{7,8},{8,9},{9,10},{10,1... | collective-permute-start | bytes 589832 | tf_op jit(solution)/shard_map/ppermute | solution.py:20
  267.5 11.2 %collective-permute-start.25 = (f32[384,128]{1,0:T(8,128)S(1)}, f32[384,128]{1,0:T(8,128)S(1)}, u32[]{:S(2)}, u32[]{:S(2)}) collective-permute-start(f32[384,128]{1,0:T(8,128)S(1)} %bitcast.1440), channel_id=1, source_target_pairs={{1,0},{2,1},{3,2},{4,3},{5,4},{6,5},{7,6},{8,7},{9,8},{10,9},{11,1... | collective-permute-start | bytes 589832 | tf_op jit(solution)/shard_map/ppermute | solution.py:20
  288.1 11.8 %collective-permute-start.26 = (f32[384,128]{1,0:T(8,128)S(1)}, f32[384,128]{1,0:T(8,128)S(1)}, u32[]{:S(2)}, u32[]{:S(2)}) collective-permute-start(f32[384,128]{1,0:T(8,128)S(1)} %bitcast.1441), channel_id=1, source_target_pairs={{0,1},{1,2},{2,3},{3,4},{4,5},{5,6},{6,7},{7,8},{8,9},{9,10},{10,1... | collective-permute-start | bytes 589832 | tf_op jit(solution)/shard_map/ppermute | solution.py:20
  290.0 11.2 %collective-permute-start.27 = (f32[384,128]{1,0:T(8,128)S(1)}, f32[384,128]{1,0:T(8,128)S(1)}, u32[]{:S(2)}, u32[]{:S(2)}) collective-permute-start(f32[384,128]{1,0:T(8,128)S(1)} %bitcast.1442), channel_id=1, source_target_pairs={{1,0},{2,1},{3,2},{4,3},{5,4},{6,5},{7,6},{8,7},{9,8},{10,9},{11,1... | collective-permute-start | bytes 589832 | tf_op jit(solution)/shard_map/ppermute | solution.py:20
  301.3 4.8 %copy-start.42 = (f32[8,8,8,128]{3,2,1,0:T(8,128)S(1)}, f32[8,8,8,128]{3,2,1,0:T(8,128)}, u32[]{:S(2)}) copy-start(f32[8,8,8,128]{3,2,1,0:T(8,128)} %get-tuple-element.208) | copy-start | bytes 786436
  301.3 4.8 %copy-start.43 = (f32[8,8,8,128]{3,2,1,0:T(8,128)S(1)}, f32[8,8,8,128]{3,2,1,0:T(8,128)}, u32[]{:S(2)}) copy-start(f32[8,8,8,128]{3,2,1,0:T(8,128)} %get-tuple-element.209) | copy-start | bytes 786436
  301.9 4.2 %copy-start.34 = (f32[8,8,8,128]{3,2,1,0:T(8,128)S(1)}, f32[8,8,8,128]{3,2,1,0:T(8,128)}, u32[]{:S(2)}) copy-start(f32[8,8,8,128]{3,2,1,0:T(8,128)} %pad_maximum_fusion.26) | copy-start | bytes 786436
  301.9 4.2 %copy-start.36 = (f32[8,8,8,128]{3,2,1,0:T(8,128)S(1)}, f32[8,8,8,128]{3,2,1,0:T(8,128)}, u32[]{:S(2)}) copy-start(f32[8,8,8,128]{3,2,1,0:T(8,128)} %pad_maximum_fusion.27) | copy-start | bytes 786436
  (85 other events, 176.5 us)
where the time goes:
time: 317 us; the launch traced here: 313 us
  starting transfers between devices  138 us (44%)
  other arithmetic  78.5 us (25%)
  local copies, waits for them, and re-layouts  68.5 us (22%)
  matrix products  15.4 us (5%)
  waiting for transfers between devices  7.22 us (2%)
  between operations  4.95 us (2%)
    ppermute x28, starting transfers between devices, from_behind(): return lax.ppermute(value, axis, pairs)  138 us
    concatenate x24, other arithmetic, neighbor_values(): jnp.concatenate([lower, lax.slice_in_dim(volume, 0, edge_len - 1, axis=di...  22.1 us
    add x8, other arithmetic, smooth(): solution = solution + update  19.9 us
    gather x11, local copies, waits for them, and re-layouts, device_ghosts(): opposite_pool = face_pool[OPPOSITE]  19 us
    slice x25, local copies, waits for them, and re-layouts, neighbor_values(): lax.slice_in_dim(volume, 0, edge_len - 1, axis=dimension)  18 us
    concatenate x19, other arithmetic, neighbor_values(): jnp.concatenate([lax.slice_in_dim(volume, 1, edge_len, axis=dimension), u...  14.2 us
    dot_general x11, matrix products, device_ghosts(): jnp.einsum('fcr,frb->fcb', opposite_pool, selector, precision=lax.Precisi...  13.3 us
    unnamed x358, local copies, waits for them, and re-layouts  8.92 us
  transfers between devices with their start and end apart: 28, of which 8 were waited for; matrix products, arithmetic and copies ran while one was open for 14% of the time, Pallas kernels for 0%

commit v1 on v0

v1 whole, which is shorter than its diff:
```python
import functools

import jax
import jax.numpy as jnp
from jax import lax
from jax.experimental import pallas as pl
from jax.experimental.pallas import tpu as pltpu
from jax.sharding import PartitionSpec as P

THETA = 1.25
DELTA = 0.75
SIGMA = THETA / DELTA
RHO0 = 1.0 / SIGMA
RHO1 = 1.0 / (2.0 * SIGMA - RHO0)
RHO2 = 1.0 / (2.0 * SIGMA - RHO1)
SWEEPS = ((0.0, 1.0 / THETA), (RHO1 * RHO0, 2.0 * RHO1 / DELTA), (RHO2 * RHO1, 2.0 * RHO2 / DELTA))

LANES = 128
FINE = 128
COARSE = 32
MESH = pl.DeviceIdType.MESH
N_COPIES = 64


def pick(values, index):
    rows = values.shape[0]
    whole = jnp.broadcast_to(index[None], (rows // 8, 8, LANES)).reshape(rows, LANES)
    return jnp.take_along_axis(values, whole, axis=1, mode="promise_in_bounds")


def pick_face(face, index):
    return pick(face.reshape(64, LANES), index).reshape(8, 8, LANES)


def kernel(
    gx, gy,
    rhs_ref, guess_ref, coef_ref, links_ref, owner_ref, ccoef_ref, clinks_ref,
    out_ref, cout_ref,
    xb, wt, bd, dg, upd, ghost, packed, recv, fidx, fmask,
    ccrow, cxb, cwt, cidg, cbd, cupd, cghost, idrow, tidx, tsrc, cidx, crec, cpack, cnidx,
    counts, src, pair2, pair2r, tall, back, backr, expand,
    ssem, rsem,
):
    devices = gx * gy
    me = lax.axis_index("gx") * gy + lax.axis_index("gy")
    valid = {1: me < devices - 1, -1: me > 0, 2: me < devices - 2, -2: me > 1}

    def device(offset):
        target = lax.rem(me + offset + devices, devices)
        return (target // gy, lax.rem(target, gy))

    barrier = pltpu.get_barrier_semaphore()
    for offset in (1, -1, 2, -2):
        @pl.when(valid[offset])
        def _():
            pl.semaphore_signal(barrier, inc=1, device_id=device(offset), device_id_type=MESH)

    used = [0]
    sent = []

    def send(offset, pairs):
        made = []
        for source, target in pairs:
            at = used[0]
            used[0] += 1
            made.append(pltpu.make_async_remote_copy(
                src_ref=source, dst_ref=target, send_sem=ssem.at[at], recv_sem=rsem.at[at],
                device_id=device(offset), device_id_type=MESH))

        @pl.when(valid[offset])
        def _():
            for copy in made:
                copy.start()

        sent.append((offset, made))
        return (offset, made)

    def arrived(handle, which=None):
        offset, made = handle

        @pl.when(valid[-offset])
        def _():
            for copy in (made if which is None else [made[which]]):
                copy.wait_recv()

    lane = lax.broadcasted_iota(jnp.int32, (8, LANES), 1)
    row = lax.broadcasted_iota(jnp.int32, (8, LANES), 0)
    row3 = lax.broadcasted_iota(jnp.int32, (8, 8, LANES), 1)
    first, last = row3 == 0, row3 == 7

    def load_cells(buffer, rows_ref):
        for c in range(4):
            block = rows_ref[:, c * LANES:(c + 1) * LANES].T
            buffer[2 * c + 1:2 * c + 3, 1:9] = block.reshape(2, 8, 8, LANES)

    def face(x, f):
        at = 1 if f % 2 == 0 else 8
        if f // 2 == 0:
            return x[at, 1:9]
        if f // 2 == 1:
            return x[1:9, at]
        return x[1:9, 1:9, 0 if f % 2 == 0 else 7]

    def put_ghost(x, g, f, value):
        at = 0 if f % 2 == 0 else 9
        if f // 2 == 0:
            x[at, 1:9] = value
        elif f // 2 == 1:
            x[1:9, at] = value
        else:
            g[f % 2] = value

    def get_ghost(x, g, f):
        at = 0 if f % 2 == 0 else 9
        if f // 2 == 0:
            return x[at, 1:9]
        if f // 2 == 1:
            return x[1:9, at]
        return g[f % 2]

    def neighbours(x, g, i):
        centre = x[i + 1, 1:9]
        low = jnp.where(first, g[0, i][:, None, :], pltpu.roll(centre, 1, 1))
        high = jnp.where(last, g[1, i][:, None, :], pltpu.roll(centre, 7, 1))
        return centre, (x[i, 1:9], x[i + 2, 1:9], x[i + 1, 0:8], x[i + 1, 2:10], low, high)

    def scaled_residual(x, g, w, b, i):
        centre, others = neighbours(x, g, i)
        total = b[i] - centre
        for f in range(6):
            total = total + w[f, i] * others[f]
        return centre, total

    def sweep(x, g, w, b, d, new, at):
        keep, gain = SWEEPS[at]

        def step(i, carry):
            centre, total = scaled_residual(x, g, w, b, i)
            update = gain * total
            if at > 0:
                update = update + keep * d[i]
            d[i] = update
            new[i + 1, 1:9] = centre + update
            return carry

        lax.fori_loop(0, 8, step, 0)

    def start_faces(e, x):
        packed[e, 0] = face(x, 4)
        packed[e, 1] = face(x, 5)
        up = send(1, [(x.at[8, 1:9], recv.at[e, 0, 0]), (x.at[1:9, 8], recv.at[e, 0, 1]), (packed.at[e, 1], recv.at[e, 0, 2])])
        down = send(-1, [(x.at[1, 1:9], recv.at[e, 1, 0]), (x.at[1:9, 1], recv.at[e, 1, 1]), (packed.at[e, 0], recv.at[e, 1, 2])])
        return up, down

    def own_ghosts(x, keep_own):
        for f in range(6):
            value = pick_face(face(x, f ^ 1), fidx[f])
            if keep_own:
                value = jnp.where(fmask[6 + f][None] != 0, value, face(x, f))
            put_ghost(x, ghost, f, value)

    def far_ghosts(e, x, handles):
        for k in range(3):
            for side in range(2):
                f = 2 * k + side
                arrived(handles[side], k)
                value = pick_face(recv[e, side, k], fidx[f])
                put_ghost(x, ghost, f, jnp.where(fmask[f][None] != 0, value, get_ghost(x, ghost, f)))

    def exchange(e, x, between=None):
        handles = start_faces(e, x)
        own_ghosts(x, False)
        if between is not None:
            between()
        far_ghosts(e, x, handles)

    coef, x0 = xb.at[0], xb.at[1]
    load_cells(coef, coef_ref)
    load_cells(x0, guess_ref)

    owner = owner_ref[...]
    to_prev = jnp.sum((owner == me - 1).astype(jnp.float32), axis=0, keepdims=True).astype(jnp.int32)
    to_next = jnp.sum((owner == me + 1).astype(jnp.float32), axis=0, keepdims=True).astype(jnp.int32)
    counts[2, 0] = jnp.broadcast_to(to_prev, (8, LANES))
    counts[2, 1] = jnp.broadcast_to(to_next, (8, LANES))
    ccrow[COARSE:2 * COARSE] = ccoef_ref[...]
    ccrow[3 * COARSE:] = jnp.ones((COARSE, 512), jnp.float32)

    pl.semaphore_wait(barrier, jnp.minimum(me, 2) + jnp.minimum(devices - 1 - me, 2))

    coef_handles = start_faces(0, coef)
    x0_handles = start_faces(1, x0)
    count_handles = [send(o, [(counts.at[2], counts.at[2 - o])]) for o in (1, -1, 2, -2)]
    ccoef_handles = [send(1, [(ccrow.at[COARSE:2 * COARSE], ccrow.at[0:COARSE])]),
                     send(-1, [(ccrow.at[COARSE:2 * COARSE], ccrow.at[2 * COARSE:3 * COARSE])])]

    links = links_ref[...].T
    for f in range(6):
        ids = jnp.broadcast_to(links[f:f + 1], (8, LANES))
        live = ids >= 0
        fidx[f] = jnp.bitwise_and(ids, FINE - 1)
        fmask[f] = jnp.where(live & (jnp.right_shift(ids, 7) != me), 1, 0)
        fmask[6 + f] = jnp.where(live, 1, 0)

    for c in range(4):
        dg[2 * c:2 * c + 2] = rhs_ref[:, c * LANES:(c + 1) * LANES].T.reshape(2, 8, 8, LANES)
    own_ghosts(coef, True)
    far_ghosts(0, coef, coef_handles)

    def weigh(x, g, w, lives, finish):
        mask4 = jnp.where((row == 0) & (lives[4] == 0), 0.0, 1.0)[None]
        mask5 = jnp.where((row == 7) & (lives[5] == 0), 0.0, 1.0)[None]

        def step(i, carry):
            centre, others = neighbours(x, g, i)
            weights = [0.5 * (centre + other) for other in others]
            diag = weights[0]
            for weight in weights[1:]:
                diag = diag + weight
            inverse = 1.0 / diag
            for f in range(6):
                value = weights[f] * inverse
                if f == 4:
                    value = value * mask4
                if f == 5:
                    value = value * mask5
                w[f, i] = value
            finish(i, diag, inverse)
            return carry

        lax.fori_loop(0, 8, step, 0)
        w[0, 0] = jnp.where(lives[0][None] != 0, w[0, 0], 0.0)
        w[1, 7] = jnp.where(lives[1][None] != 0, w[1, 7], 0.0)
        w[2, :, 0] = jnp.where(lives[2][None] != 0, w[2, :, 0], 0.0)
        w[3, :, 7] = jnp.where(lives[3][None] != 0, w[3, :, 7], 0.0)

    def fine_finish(i, diag, inverse):
        bd[i] = dg[i] * inverse
        dg[i] = diag

    weigh(coef, ghost, wt, [fmask[6 + f] for f in range(6)], fine_finish)

    own_ghosts(x0, False)
    far_ghosts(1, x0, x0_handles)
    sweep(x0, ghost, wt, bd, upd, xb.at[2], 0)

    own_lane = (jnp.right_shift(lane, 5) == 1)
    group = jnp.right_shift(lane, 5)
    slot = jnp.bitwise_and(lane, COARSE - 1)
    coarse_handles = []

    def coarse_setup_a():
        for handle in ccoef_handles + count_handles:
            arrived(handle)
        load_cells(cxb.at[0], ccrow)
        zeros = jnp.zeros((COARSE, 6), jnp.int32)
        links_c = jnp.concatenate([zeros, clinks_ref[...], zeros, zeros], axis=0).T
        lives = []
        x = cxb.at[0]
        for f in range(6):
            ids = jnp.broadcast_to(links_c[f:f + 1], (8, LANES))
            live = ids >= 0
            step_by = jnp.right_shift(ids, 5) - me
            place = jnp.bitwise_and((step_by + 1) * COARSE + jnp.bitwise_and(ids, COARSE - 1), LANES - 1)
            place = jnp.where(own_lane & live, place, lane)
            cidx[f] = place
            cnidx[f] = jnp.bitwise_and(ids, COARSE - 1) + (f // 2) * COARSE
            cnidx[6 + f] = jnp.where(own_lane & live & (step_by != 0), 1, 0)
            lives.append(jnp.where(live, 1, 0))
            value = jnp.where(live[None], pick_face(face(x, f ^ 1), place), face(x, f))
            put_ghost(x, cghost, f, value)

        def finish(i, diag, inverse):
            cidg[i] = inverse

        weigh(x, cghost, cwt, lives, finish)
        for c in range(4):
            block = cidg[2 * c:2 * c + 2].reshape(LANES, LANES).T
            idrow[COARSE:2 * COARSE, c * LANES:(c + 1) * LANES] = block[COARSE:2 * COARSE]
        coarse_handles.append(send(1, [(idrow.at[COARSE:2 * COARSE], idrow.at[0:COARSE])]))
        coarse_handles.append(send(-1, [(idrow.at[COARSE:2 * COARSE], idrow.at[2 * COARSE:3 * COARSE])]))

    def known(k, which):
        return counts[k, which] if k == 2 else jnp.where(valid[k - 2], counts[k, which], 0)

    def by_group(values):
        return jnp.where(group == 0, values[0], jnp.where(group == 1, values[1], values[2]))

    def coarse_setup_b():
        a = [known(k, 0) for k in range(5)]
        n = [known(k, 1) for k in range(5)]
        stay = [FINE - a[k] - n[k] if k == 2 else jnp.where(valid[k - 2], FINE - a[k] - n[k], 0) for k in range(5)]
        before, here = by_group(n[0:3]), by_group(stay[1:4])
        start, after = by_group(a[1:4]), by_group(a[2:5])
        for o in range(4):
            rank = 8 * slot + 2 * o + jnp.where(row >= 4, 1, 0)
            in_before = rank < before
            in_here = rank < before + here
            in_after = rank < before + here + after
            at = jnp.where(in_before, FINE - before + rank, jnp.where(in_here, start + rank - before, rank - before - here))
            step_by = jnp.where(in_before, group - 2, jnp.where(in_here, group - 1, group))
            source = jnp.where((step_by == 2) | (step_by == -2), 0, step_by + 2)
            tidx[o] = jnp.bitwise_and(at, LANES - 1)
            tsrc[o] = jnp.where(in_after & (group < 3), source, 4)
        rank_own = n[1] + lane - a[2]
        rank_far = jnp.where(lane < 64, n[1] + stay[2] + lane, lane - FINE + n[1])
        for k, rank in enumerate((rank_own, rank_far)):
            rank = jnp.bitwise_and(rank, 255)
            tidx[4 + 2 * k] = COARSE + jnp.right_shift(rank, 3)
            tidx[5 + 2 * k] = jnp.bitwise_and(rank, 7)

    def coarse_setup_c():
        for handle in coarse_handles:
            arrived(handle)
        for c in range(4):
            block = idrow[:, c * LANES:(c + 1) * LANES].T
            cidg[2 * c:2 * c + 2] = block.reshape(2, 8, 8, LANES)

    exchange(2, xb.at[2], coarse_setup_a)
    sweep(xb.at[2], ghost, wt, bd, upd, xb.at[3], 1)
    exchange(3, xb.at[3], coarse_setup_b)
    sweep(xb.at[3], ghost, wt, bd, upd, xb.at[4], 2)
    exchange(4, xb.at[4], coarse_setup_c)

    x3 = xb.at[4]

    def restrict_step(i, carry):
        total = jnp.zeros((4, 8, LANES), jnp.float32)
        for half in range(2):
            _, scaled = scaled_residual(x3, ghost, wt, bd, 2 * i + half)
            quads = (scaled * dg[2 * i + half]).reshape(4, 2, 8, LANES)
            total = total + quads[:, 0] + quads[:, 1]
        total = total + pltpu.roll(total, 7, 1)
        tall[pl.ds(pl.multiple_of(i * 32, 32), 32)] = 0.5 * total.reshape(32, LANES)
        return carry

    lax.fori_loop(0, 4, restrict_step, 0)
    restricted = tall[pl.ds(0, 64, stride=2)]
    src[2] = restricted
    low_lane = jnp.broadcast_to((lane < 64)[None], (4, 8, LANES)).reshape(32, LANES)
    turned = pltpu.roll(restricted[32:], 64, 1)
    pair2[0] = jnp.where(low_lane, turned, restricted[:32])
    pair2[1] = jnp.where(low_lane, restricted[:32], turned)
    r_handles = [send(1, [(src.at[2], src.at[1])]), send(-1, [(src.at[2], src.at[3])]),
                 send(2, [(pair2.at[0], pair2r.at[0])]), send(-2, [(pair2.at[1], pair2r.at[1])])]
    for handle in r_handles:
        arrived(handle)
    src[0, 0:32] = jnp.where(low_lane, pair2r[1], pair2r[0])
    src[0, 32:64] = pltpu.roll(jnp.where(low_lane, pair2r[0], pair2r[1]), 64, 1)

    for o in range(4):
        ox, oy = o // 2, o % 2
        index, which = tidx[o], tsrc[o]
        for i in range(4):
            for j in range(4):
                q = 4 * (4 * i + j)
                value = jnp.zeros((8, LANES), jnp.float32)
                for k in range(4):
                    four = src[k, q:q + 4]
                    taken = pick(jnp.concatenate([four, four], axis=0), index)
                    value = jnp.where(which == k, taken, value)
                at = (4 * ox + i, 4 * oy + j)
                scaled = value * cidg[at[0], at[1]]
                cbd[at[0], at[1]] = scaled
                update = scaled * (1.0 / THETA)
                cupd[at[0], at[1]] = update
                cxb[1, at[0] + 1, at[1] + 1] = update

    c1, c2, c3 = cxb.at[1], cxb.at[2], cxb.at[3]
    for f in range(6):
        put_ghost(c1, cghost, f, pick_face(face(c1, f ^ 1), cidx[f]))
    sweep(c1, cghost, cwt, cbd, cupd, c2, 1)

    lane64 = jnp.broadcast_to(lane[None], (8, 8, LANES)).reshape(64, LANES)
    for side in range(2):
        faces = [face(c2, 2 * k + side).reshape(64, LANES) for k in range(3)]
        cpack[side] = jnp.where(lane64 < 32, pltpu.roll(faces[0], 96, 1), jnp.where(lane64 < 64, faces[1], pltpu.roll(faces[2], 32, 1)))
    c_handles = [send(1, [(cpack.at[1], crec.at[0])]), send(-1, [(cpack.at[0], crec.at[1])])]
    for f in range(6):
        put_ghost(c2, cghost, f, pick_face(face(c2, f ^ 1), cidx[f]))
    for side in range(2):
        arrived(c_handles[side])
        for k in range(3):
            f = 2 * k + side
            value = pick(crec[side], cnidx[f]).reshape(8, 8, LANES)
            put_ghost(c2, cghost, f, jnp.where(cnidx[6 + f][None] != 0, value, get_ghost(c2, cghost, f)))
    sweep(c2, cghost, cwt, cbd, cupd, c3, 2)

    for k in (1, 0):
        place, octant = tidx[4 + 2 * k], tidx[5 + 2 * k]
        straight = (jnp.bitwise_and(octant, 1) == 0) == (row < 4)
        outer = jnp.right_shift(octant, 1)
        for i in range(4):
            quads = []
            for j in range(4):
                value = pick(c3[i + 1, j + 1], place)
                for o in range(1, 4):
                    value = jnp.where(outer == o, pick(c3[4 * (o // 2) + i + 1, 4 * (o % 2) + j + 1], place), value)
                quads.append(jnp.where(straight, value, pltpu.roll(value, 4, 0)))
            for half in range(2):
                at = 16 * i + 8 * half
                back[k, at:at + 8] = jnp.where(row < 4, quads[2 * half], quads[2 * half + 1])
        if k == 1:
            b_handles = [send(1, [(back.at[1], backr.at[0])]), send(-1, [(back.at[1], backr.at[1])])]
    for c in range(4):
        block = c3[2 * c + 1:2 * c + 3, 1:9].reshape(LANES, LANES).T
        cout_ref[:, c * LANES:(c + 1) * LANES] = block[COARSE:2 * COARSE]
    for handle in b_handles:
        arrived(handle)
    from_prev = jnp.where(lane < counts[2, 0], 1, 0)
    from_next = jnp.where(lane >= FINE - counts[2, 1], 1, 0)
    from_prev = jnp.broadcast_to(from_prev[None], (8, 8, LANES)).reshape(64, LANES)
    from_next = jnp.broadcast_to(from_next[None], (8, 8, LANES)).reshape(64, LANES)
    values = jnp.where(from_prev != 0, backr[0], jnp.where(from_next != 0, backr[1], back[0]))
    expand[pl.ds(0, 64, stride=2)] = values
    expand[pl.ds(1, 64, stride=2)] = values

    def correct_step(i, carry):
        four = expand[pl.ds(pl.multiple_of((i // 2) * 32, 32), 32)].reshape(4, 1, 8, LANES)
        xb[5, i + 1, 1:9] = x3[i + 1, 1:9] + jnp.broadcast_to(four, (4, 2, 8, LANES)).reshape(8, 8, LANES)
        return carry

    lax.fori_loop(0, 8, correct_step, 0)

    for at in range(3):
        exchange(5 + at, xb.at[5 + at])
        sweep(xb.at[5 + at], ghost, wt, bd, upd, xb.at[6 + at], at)
    for c in range(4):
        block = xb[8, 2 * c + 1:2 * c + 3, 1:9].reshape(LANES, LANES).T
        out_ref[:, c * LANES:(c + 1) * LANES] = block

    for offset in (1, -1, 2, -2):
        @pl.when(valid[offset])
        def _():
            for o, made in sent:
                if o == offset:
                    for copy in made:
                        copy.wait_send()


def solution(mesh):
    gx, gy = mesh.shape["gx"], mesh.shape["gy"]
    f32, i32 = jnp.float32, jnp.int32

    def on_device(*args):
        whole = pl.BlockSpec(memory_space=pltpu.VMEM)
        volume, padded = (8, 8, 8, LANES), (10, 10, 8, LANES)
        return pl.pallas_call(
            functools.partial(kernel, gx, gy),
            out_shape=(jax.ShapeDtypeStruct((FINE, 512), f32), jax.ShapeDtypeStruct((COARSE, 512), f32)),
            in_specs=[whole] * 7,
            out_specs=(whole, whole),
            scratch_shapes=[
                pltpu.VMEM((9,) + padded, f32),
                pltpu.VMEM((6,) + volume, f32),
                pltpu.VMEM(volume, f32),
                pltpu.VMEM(volume, f32),
                pltpu.VMEM(volume, f32),
                pltpu.VMEM((2, 8, 8, LANES), f32),
                pltpu.VMEM((8, 2, 8, 8, LANES), f32),
                pltpu.VMEM((8, 2, 3, 8, 8, LANES), f32),
                pltpu.VMEM((6, 8, LANES), i32),
                pltpu.VMEM((12, 8, LANES), i32),
                pltpu.VMEM((LANES, 512), f32),
                pltpu.VMEM((4,) + padded, f32),
                pltpu.VMEM((6,) + volume, f32),
                pltpu.VMEM(volume, f32),
                pltpu.VMEM(volume, f32),
                pltpu.VMEM(volume, f32),
                pltpu.VMEM((2, 8, 8, LANES), f32),
                pltpu.VMEM((LANES, 512), f32),
                pltpu.VMEM((8, 8, LANES), i32),
                pltpu.VMEM((4, 8, LANES), i32),
                pltpu.VMEM((6, 8, LANES), i32),
                pltpu.VMEM((2, 64, LANES), f32),
                pltpu.VMEM((2, 64, LANES), f32),
                pltpu.VMEM((12, 8, LANES), i32),
                pltpu.VMEM((5, 2, 8, LANES), i32),
                pltpu.VMEM((4, 64, LANES), f32),
                pltpu.VMEM((2, 32, LANES), f32),
                pltpu.VMEM((2, 32, LANES), f32),
                pltpu.VMEM((LANES, LANES), f32),
                pltpu.VMEM((2, 64, LANES), f32),
                pltpu.VMEM((2, 64, LANES), f32),
                pltpu.VMEM((LANES, LANES), f32),
                pltpu.SemaphoreType.DMA((N_COPIES,)),
                pltpu.SemaphoreType.DMA((N_COPIES,)),
            ],
            compiler_params=pltpu.CompilerParams(collective_id=0, has_side_effects=True, vmem_limit_bytes=40 * 1024 * 1024),
        )(*args)

    rows = P(("gx", "gy"), None)
    return jax.shard_map(on_device, mesh=mesh, in_specs=(rows,) * 7, out_specs=(rows, rows), check_vma=False)
```

time: 317 us -> 70 us (0.22); the launches traced: 313 us -> 69.4 us
  starting transfers between devices: 138 us -> 0 us
  other arithmetic: 78.5 us -> 0 us
  Pallas kernels: 0 us -> 63 us
  local copies, waits for them, and re-layouts: 68.5 us -> 5.81 us
  matrix products: 15.4 us -> 0 us
  waiting for transfers between devices: 7.22 us -> 0 us
  between operations: 4.95 us -> 0.66 us
    ppermute x28 -> x0, starting transfers between devices: 138 us -> none  [from_behind(): return lax.ppermute(value, axis, pairs)]
    pallas_call x0 -> x1, Pallas kernels: none -> 63 us  [on_device(): pl.pallas_call(functools.partial(kernel, gx, gy), out_shape=(jax.ShapeDty...]
    concatenate x55 -> x0, other arithmetic: 45.2 us -> none  [the longest x24 22.1 us: neighbor_values(): jnp.concatenate([lower, lax.slice_in_dim(volume, 0, edge_len - 1, axis=di...]
    slice x66 -> x0, local copies, waits for them, and re-layouts: 37.5 us -> none  [the longest x25 18 us: neighbor_values(): lax.slice_in_dim(volume, 0, edge_len - 1, axis=dimension)]
    add x9 -> x0, other arithmetic: 19.9 us -> none  [the longest x8 19.9 us: smooth(): solution = solution + update]
    gather x11 -> x0, local copies, waits for them, and re-layouts: 19 us -> none  [device_ghosts(): opposite_pool = face_pool[OPPOSITE]]
    dot_general x19 -> x0, matrix products: 15.4 us -> none  [the longest x11 13.3 us: device_ghosts(): jnp.einsum('fcr,frb->fcb', opposite_pool, selector, precision=lax.Precisi...]
    reduce_sum x5 -> x0, other arithmetic: 7.38 us -> none  [the longest x1 5.81 us: restrict(): residual.reshape(half, 2, half, 2, half, 2, count).sum(axis=(1, 3, 5)) * 0.5]
  transfers between devices with their start and end apart: 28 -> 0, of which waited for: 8 -> 0; matrix products, arithmetic and copies ran while one was open for 14% -> 0% of each run, Pallas kernels for 0% -> 0%
where the time goes in v1:
time: 70 us; the launch traced here: 69.4 us
  Pallas kernels  63 us (90%)
  local copies, waits for them, and re-layouts  5.81 us (8%)
    pallas_call x1, Pallas kernels, on_device(): pl.pallas_call(functools.partial(kernel, gx, gy), out_shape=(jax.ShapeDty...  63 us
    unnamed x17, local copies, waits for them, and re-layouts  5.81 us

profile of v1, /device:TPU:32, one launch (start us, length us, event | category | flops | bytes accessed | tf_op | source)
XLA Modules:
  0.0 69.4 jit_solution(13691710008461852073)
XLA Ops:
  0.6 0.0 copy-start.4
  0.6 0.8 %copy.11.clinks_ref = s32[32,6]{1,0:T(8,128)S(1)} copy(s32[32,6]{0,1:T(8,128)} %param.13) | data formatting | bytes 1536 | tf_op args[6]
  1.4 0.0 copy-done.4
  1.4 0.0 copy-start.5
  1.4 0.0 copy-start.3
  1.4 0.1 copy.9.links_ref
  1.5 0.5 copy-done.5
  2.1 0.1 copy.10.owner_ref
  2.2 0.1 copy-done.3
  2.3 0.0 copy-start
  2.3 0.9 %copy-done = f32[128,512]{1,0:T(8,128)S(1)} copy-done((f32[128,512]{1,0:T(8,128)S(1)}, f32[128,512]{1,0:T(8,128)}, u32[]{:S(2)}) %copy-start) | copy-done | bytes 262168
  3.2 0.0 copy-start.1
  3.2 0.9 %copy-done.1 = f32[128,512]{1,0:T(8,128)S(1)} copy-done((f32[128,512]{1,0:T(8,128)S(1)}, f32[128,512]{1,0:T(8,128)}, u32[]{:S(2)}) %copy-start.1) | copy-done | bytes 262168
  4.2 0.0 copy-start.2
  4.2 0.9 %copy-done.2 = f32[128,512]{1,0:T(8,128)S(1)} copy-done((f32[128,512]{1,0:T(8,128)S(1)}, f32[128,512]{1,0:T(8,128)}, u32[]{:S(2)}) %copy-start.2) | copy-done | bytes 262168
  5.1 63.0 %shard_map.86 = (f32[128,512]{1,0:T(8,128)S(1)}, f32[32,512]{1,0:T(8,128)S(1)}) custom-call(f32[128,512]{1,0:T(8,128)S(1)} %copy-done, f32[128,512]{1,0:T(8,128)S(1)} %copy-done.1, f32[128,512]{1,0:T(8,128)S(1)} %copy-done.2, s32[128,6]{1,0:T(8,128)S(1)} %copy.9.links_ref, s32[128,1]{1,0:T(8,128)S(1)} %copy.10.owner_ref, f32[32,512]{1,0:T(8,128)S(1)} %copy-done.3, ...), custom_call_target="tpu_custom_call" | custom-call | tf_op jit(solution)/shard_map/pallas_call | solution.py:448
  68.1 0.7 %copy.14 = f32[128,512]{1,0:T(8,128)} copy(f32[128,512]{1,0:T(8,128)S(1)} %get-tuple-element.4) | data formatting | bytes 524288
  68.8 0.6 copy.15
Async XLA Ops:
  0.6 0.8 %copy-start.4 = (s32[128,6]{0,1:T(8,128)S(1)}, s32[128,6]{0,1:T(8,128)}, u32[]{:S(2)}) copy-start(s32[128,6]{0,1:T(8,128)} %param.10) | copy-start | bytes 9220
  1.4 0.7 copy-start.5
  1.4 0.9 %copy-start.3 = (f32[32,512]{1,0:T(8,128)S(1)}, f32[32,512]{1,0:T(8,128)}, u32[]{:S(2)}) copy-start(f32[32,512]{1,0:T(8,128)} %ccoef_ref.1) | copy-start | bytes 196612
  2.3 0.9 %copy-start = (f32[128,512]{1,0:T(8,128)S(1)}, f32[128,512]{1,0:T(8,128)}, u32[]{:S(2)}) copy-start(f32[128,512]{1,0:T(8,128)} %rhs_ref.1) | copy-start | bytes 786436
  3.2 0.9 %copy-start.1 = (f32[128,512]{1,0:T(8,128)S(1)}, f32[128,512]{1,0:T(8,128)}, u32[]{:S(2)}) copy-start(f32[128,512]{1,0:T(8,128)} %guess_ref.1) | copy-start | bytes 786436
  4.2 0.9 %copy-start.2 = (f32[128,512]{1,0:T(8,128)S(1)}, f32[128,512]{1,0:T(8,128)}, u32[]{:S(2)}) copy-start(f32[128,512]{1,0:T(8,128)} %coef_ref.1) | copy-start | bytes 786436

commit v2 on v1

--- a/solution.py
+++ b/solution.py
@@ -34,12 +34,13 @@
 
 def kernel(
     gx, gy,
-    rhs_ref, guess_ref, coef_ref, links_ref, owner_ref, ccoef_ref, clinks_ref,
+    rhs_hbm, guess_hbm, coef_hbm, links_hbm, owner_hbm, ccoef_hbm, clinks_hbm,
     out_ref, cout_ref,
+    rhs_ref, guess_ref, coef_ref, links_ref, owner_ref, clinks_ref,
     xb, wt, bd, dg, upd, ghost, packed, recv, fidx, fmask,
     ccrow, cxb, cwt, cidg, cbd, cupd, cghost, idrow, tidx, tsrc, cidx, crec, cpack, cnidx,
     counts, src, pair2, pair2r, tall, back, backr, expand,
-    ssem, rsem,
+    ssem, rsem, isem,
 ):
     devices = gx * gy
     me = lax.axis_index("gx") * gy + lax.axis_index("gy")
@@ -54,6 +55,13 @@
         @pl.when(valid[offset])
         def _():
             pl.semaphore_signal(barrier, inc=1, device_id=device(offset), device_id_type=MESH)
+
+    fetches = []
+    for at, (source, target) in enumerate((
+            (coef_hbm, coef_ref), (guess_hbm, guess_ref), (owner_hbm, owner_ref), (links_hbm, links_ref),
+            (ccoef_hbm, ccrow.at[COARSE:2 * COARSE]), (rhs_hbm, rhs_ref), (clinks_hbm, clinks_ref))):
+        fetches.append(pltpu.make_async_copy(source, target, isem.at[at]))
+        fetches[-1].start()
 
     used = [0]
     sent = []
@@ -143,7 +151,7 @@
             new[i + 1, 1:9] = centre + update
             return carry
 
-        lax.fori_loop(0, 8, step, 0)
+        lax.fori_loop(0, 8, step, 0, unroll=True)
 
     def start_faces(e, x):
         packed[e, 0] = face(x, 4)
@@ -160,10 +168,11 @@
             put_ghost(x, ghost, f, value)
 
     def far_ghosts(e, x, handles):
+        for side in range(2):
+            arrived(handles[side])
         for k in range(3):
             for side in range(2):
                 f = 2 * k + side
-                arrived(handles[side], k)
                 value = pick_face(recv[e, side, k], fidx[f])
                 put_ghost(x, ghost, f, jnp.where(fmask[f][None] != 0, value, get_ghost(x, ghost, f)))
 
@@ -175,15 +184,18 @@
         far_ghosts(e, x, handles)
 
     coef, x0 = xb.at[0], xb.at[1]
+    fetches[0].wait()
     load_cells(coef, coef_ref)
+    fetches[1].wait()
     load_cells(x0, guess_ref)
+    for fetch in fetches[2:]:
+        fetch.wait()
 
     owner = owner_ref[...]
-    to_prev = jnp.sum((owner == me - 1).astype(jnp.float32), axis=0, keepdims=True).astype(jnp.int32)
-    to_next = jnp.sum((owner == me + 1).astype(jnp.float32), axis=0, keepdims=True).astype(jnp.int32)
+    to_prev = jnp.sum((owner == me - 1).astype(jnp.float32), axis=1, keepdims=True).astype(jnp.int32)
+    to_next = jnp.sum((owner == me + 1).astype(jnp.float32), axis=1, keepdims=True).astype(jnp.int32)
     counts[2, 0] = jnp.broadcast_to(to_prev, (8, LANES))
     counts[2, 1] = jnp.broadcast_to(to_next, (8, LANES))
-    ccrow[COARSE:2 * COARSE] = ccoef_ref[...]
     ccrow[3 * COARSE:] = jnp.ones((COARSE, 512), jnp.float32)
 
     pl.semaphore_wait(barrier, jnp.minimum(me, 2) + jnp.minimum(devices - 1 - me, 2))
@@ -194,7 +206,7 @@
     ccoef_handles = [send(1, [(ccrow.at[COARSE:2 * COARSE], ccrow.at[0:COARSE])]),
                      send(-1, [(ccrow.at[COARSE:2 * COARSE], ccrow.at[2 * COARSE:3 * COARSE])])]
 
-    links = links_ref[...].T
+    links = links_ref[...]
     for f in range(6):
         ids = jnp.broadcast_to(links[f:f + 1], (8, LANES))
         live = ids >= 0
@@ -228,7 +240,7 @@
             finish(i, diag, inverse)
             return carry
 
-        lax.fori_loop(0, 8, step, 0)
+        lax.fori_loop(0, 8, step, 0, unroll=True)
         w[0, 0] = jnp.where(lives[0][None] != 0, w[0, 0], 0.0)
         w[1, 7] = jnp.where(lives[1][None] != 0, w[1, 7], 0.0)
         w[2, :, 0] = jnp.where(lives[2][None] != 0, w[2, :, 0], 0.0)
@@ -253,8 +265,8 @@
         for handle in ccoef_handles + count_handles:
             arrived(handle)
         load_cells(cxb.at[0], ccrow)
-        zeros = jnp.zeros((COARSE, 6), jnp.int32)
-        links_c = jnp.concatenate([zeros, clinks_ref[...], zeros, zeros], axis=0).T
+        zeros = jnp.zeros((6, COARSE), jnp.int32)
+        links_c = jnp.concatenate([zeros, clinks_ref[...], zeros, zeros], axis=1)
         lives = []
         x = cxb.at[0]
         for f in range(6):
@@ -334,7 +346,7 @@
         tall[pl.ds(pl.multiple_of(i * 32, 32), 32)] = 0.5 * total.reshape(32, LANES)
         return carry
 
-    lax.fori_loop(0, 4, restrict_step, 0)
+    lax.fori_loop(0, 4, restrict_step, 0, unroll=True)
     restricted = tall[pl.ds(0, 64, stride=2)]
     src[2] = restricted
     low_lane = jnp.broadcast_to((lane < 64)[None], (4, 8, LANES)).reshape(32, LANES)
@@ -420,7 +432,7 @@
         xb[5, i + 1, 1:9] = x3[i + 1, 1:9] + jnp.broadcast_to(four, (4, 2, 8, LANES)).reshape(8, 8, LANES)
         return carry
 
-    lax.fori_loop(0, 8, correct_step, 0)
+    lax.fori_loop(0, 8, correct_step, 0, unroll=True)
 
     for at in range(3):
         exchange(5 + at, xb.at[5 + at])
@@ -442,15 +454,21 @@
     gx, gy = mesh.shape["gx"], mesh.shape["gy"]
     f32, i32 = jnp.float32, jnp.int32
 
-    def on_device(*args):
+    def on_device(rhs, guess, coef, links, owner, ccoef, clinks):
         whole = pl.BlockSpec(memory_space=pltpu.VMEM)
         volume, padded = (8, 8, 8, LANES), (10, 10, 8, LANES)
         return pl.pallas_call(
             functools.partial(kernel, gx, gy),
             out_shape=(jax.ShapeDtypeStruct((FINE, 512), f32), jax.ShapeDtypeStruct((COARSE, 512), f32)),
-            in_specs=[whole] * 7,
+            in_specs=[pl.BlockSpec(memory_space=pltpu.HBM)] * 7,
             out_specs=(whole, whole),
             scratch_shapes=[
+                pltpu.VMEM((FINE, 512), f32),
+                pltpu.VMEM((FINE, 512), f32),
+                pltpu.VMEM((FINE, 512), f32),
+                pltpu.VMEM((6, FINE), i32),
+                pltpu.VMEM((1, FINE), i32),
+                pltpu.VMEM((6, COARSE), i32),
                 pltpu.VMEM((9,) + padded, f32),
                 pltpu.VMEM((6,) + volume, f32),
                 pltpu.VMEM(volume, f32),
@@ -485,9 +503,10 @@
                 pltpu.VMEM((LANES, LANES), f32),
                 pltpu.SemaphoreType.DMA((N_COPIES,)),
                 pltpu.SemaphoreType.DMA((N_COPIES,)),
+                pltpu.SemaphoreType.DMA((7,)),
             ],
-            compiler_params=pltpu.CompilerParams(collective_id=0, has_side_effects=True, vmem_limit_bytes=40 * 1024 * 1024),
-        )(*args)
+            compiler_params=pltpu.CompilerParams(collective_id=0, has_side_effects=True, vmem_limit_bytes=56 * 1024 * 1024),
+        )(rhs, guess, coef, links.T, owner.T, ccoef, clinks.T)
 
     rows = P(("gx", "gy"), None)
     return jax.shard_map(on_device, mesh=mesh, in_specs=(rows,) * 7, out_specs=(rows, rows), check_vma=False)

time: 70 us -> 65.9 us (0.941)
  local copies, waits for them, and re-layouts: 5.81 us -> 2.34 us
    unnamed x17 -> x4, local copies, waits for them, and re-layouts: 5.81 us -> 2.34 us
where the time goes in v2:
time: 65.9 us; the launch traced here: 65.4 us
  Pallas kernels  62.4 us (95%)
  local copies, waits for them, and re-layouts  2.34 us (4%)
    pallas_call x1, Pallas kernels, on_device(): pl.pallas_call(functools.partial(kernel, gx, gy), out_shape=(jax.ShapeDty...  62.4 us
    unnamed x4, local copies, waits for them, and re-layouts  2.34 us

profile of v2, /device:TPU:32, one launch (start us, length us, event | category | flops | bytes accessed | tf_op | source)
XLA Modules:
  0.0 65.4 jit_solution(7822821653913272727)
XLA Ops:
  0.6 62.4 %shard_map.86 = (f32[128,512]{1,0:T(8,128)}, f32[32,512]{1,0:T(8,128)}) custom-call(f32[128,512]{1,0:T(8,128)} %rhs_hbm.1, f32[128,512]{1,0:T(8,128)} %guess_hbm.1, f32[128,512]{1,0:T(8,128)} %coef_hbm.1, s32[6,128]{1,0:T(8,128)} %bitcast.3, s32[1,128]{1,0:T(1,128)} %bitcast.5, f32[32,512]{1,0:T(8,128)} %ccoef_hbm.1, s32[6,32]{1,0:T(8,128)} %bitcast.4), custom_call_target="tpu_custom_call" | custom-call | tf_op jit(solution)/shard_map/pallas_call | solution.py:460
  63.1 0.0 copy-start
  63.1 1.7 %copy.11 = f32[128,512]{1,0:T(8,128)} copy(f32[128,512]{1,0:T(8,128)} %get-tuple-element.4) | data formatting | bytes 524288
  64.8 0.0 copy-done
  64.8 0.6 copy.12
Async XLA Ops:
  63.1 1.7 %copy-start = (f32[32,512]{1,0:T(8,128)S(1)}, f32[32,512]{1,0:T(8,128)}, u32[]{:S(2)}) copy-start(f32[32,512]{1,0:T(8,128)} %get-tuple-element.5) | copy-start | bytes 196612

commit v3 on v2

--- a/solution.py
+++ b/solution.py
@@ -19,7 +19,7 @@
 FINE = 128
 COARSE = 32
 MESH = pl.DeviceIdType.MESH
-N_COPIES = 64
+N_COPIES = 96
 
 
 def pick(values, index):
@@ -39,7 +39,8 @@
     rhs_ref, guess_ref, coef_ref, links_ref, owner_ref, clinks_ref,
     xb, wt, bd, dg, upd, ghost, packed, recv, fidx, fmask,
     ccrow, cxb, cwt, cidg, cbd, cupd, cghost, idrow, tidx, tsrc, cidx, crec, cpack, cnidx,
-    counts, src, pair2, pair2r, tall, back, backr, expand,
+    counts, src, pair2, pair2r, tall, back, backr, expand, near, expand2, ghost2,
+    nlinks, nidx, nmask, wface, flux, edges, erecv, beside, ghost3,
     ssem, rsem, isem,
 ):
     devices = gx * gy
@@ -139,7 +140,7 @@
             total = total + w[f, i] * others[f]
         return centre, total
 
-    def sweep(x, g, w, b, d, new, at):
+    def sweep(x, g, w, b, d, new, at, final=True):
         keep, gain = SWEEPS[at]
 
         def step(i, carry):
@@ -147,7 +148,8 @@
             update = gain * total
             if at > 0:
                 update = update + keep * d[i]
-            d[i] = update
+            if final:
+                d[i] = update
             new[i + 1, 1:9] = centre + update
             return carry
 
@@ -160,28 +162,79 @@
         down = send(-1, [(x.at[1, 1:9], recv.at[e, 1, 0]), (x.at[1:9, 1], recv.at[e, 1, 1]), (packed.at[e, 0], recv.at[e, 1, 2])])
         return up, down
 
-    def own_ghosts(x, keep_own):
+    def own_ghosts(x, g, keep_own=False, zero_far=False):
         for f in range(6):
             value = pick_face(face(x, f ^ 1), fidx[f])
             if keep_own:
                 value = jnp.where(fmask[6 + f][None] != 0, value, face(x, f))
-            put_ghost(x, ghost, f, value)
-
-    def far_ghosts(e, x, handles):
-        for side in range(2):
-            arrived(handles[side])
+            if zero_far:
+                value = jnp.where(fmask[f][None] != 0, 0.0, value)
+            put_ghost(x, g, f, value)
+
+    def far_ghosts(faces, x, g, handles=()):
+        for handle in handles:
+            arrived(handle)
         for k in range(3):
             for side in range(2):
                 f = 2 * k + side
-                value = pick_face(recv[e, side, k], fidx[f])
-                put_ghost(x, ghost, f, jnp.where(fmask[f][None] != 0, value, get_ghost(x, ghost, f)))
-
-    def exchange(e, x, between=None):
+                value = pick_face(faces[side, k], fidx[f])
+                put_ghost(x, g, f, jnp.where(fmask[f][None] != 0, value, get_ghost(x, g, f)))
+
+    def across(k, m):
+        return (m if m < k else m - 1)
+
+    def line(k, m, at):
+        return (at,) if across(k, m) == 0 else (slice(None), at)
+
+    def two_sweeps(x, g, middle, g_middle, new, partial, e, between=None):
+        keep, gain = SWEEPS[1]
         handles = start_faces(e, x)
-        own_ghosts(x, False)
+        for side in range(2):
+            for k in range(3):
+                f = 2 * k + side
+                value = pick_face(face(x, f) * wface[f], nidx[side, k])
+                flux[side, k] = jnp.where(nmask[side, k][None] != 0, value, 0.0)
+        at = 0
+        for m in range(3):
+            for k in range(3):
+                if k != m:
+                    for side in range(2):
+                        edges[e // 7, side, at] = flux[(side, m) + line(m, k, 7 if side else 0)]
+                    at += 1
+        edge_handles = [send(2, [(edges.at[e // 7, 1], erecv.at[e // 7, 0])]), send(-2, [(edges.at[e // 7, 0], erecv.at[e // 7, 1])])]
+        own_ghosts(x, g, zero_far=True)
+        sweep(x, g, wt, bd, upd, partial, 1, final=False)
+        partial_handles = start_faces(e + 1, partial)
+        for side in range(2):
+            end = 0 if side else 7
+            for k in range(3):
+                beside[side, k] = flux[side, k]
+                for m in range(3):
+                    if m != k:
+                        where = (side, k) + line(k, m, end)
+                        beside[where] = beside[where] + flux[(side, m) + line(m, k, end)]
         if between is not None:
             between()
-        far_ghosts(e, x, handles)
+        far_ghosts(recv.at[e], x, g, handles)
+        sweep(x, g, wt, bd, upd, middle, 1)
+        own_ghosts(middle, g_middle)
+        for handle in edge_handles + list(partial_handles):
+            arrived(handle)
+        for side in range(2):
+            end = 0 if side else 7
+            at = 0
+            for m in range(3):
+                for k in range(3):
+                    if k != m:
+                        where = (side, k) + line(k, m, 7 - end)
+                        behind = jnp.where(valid[2 if side else -2], erecv[e // 7, side, at], 0.0)
+                        beside[where] = beside[where] + behind
+                        at += 1
+        for side in range(2):
+            for k in range(3):
+                beside[side, k] = recv[e + 1, side, k] + gain * recv[3, side, k] * beside[side, k]
+        far_ghosts(beside, middle, g_middle)
+        sweep(middle, g_middle, wt, bd, upd, new, 2)
 
     coef, x0 = xb.at[0], xb.at[1]
     fetches[0].wait()
@@ -203,6 +256,7 @@
     coef_handles = start_faces(0, coef)
     x0_handles = start_faces(1, x0)
     count_handles = [send(o, [(counts.at[2], counts.at[2 - o])]) for o in (1, -1, 2, -2)]
+    link_handles = [send(1, [(links_ref, nlinks.at[0])]), send(-1, [(links_ref, nlinks.at[1])])]
     ccoef_handles = [send(1, [(ccrow.at[COARSE:2 * COARSE], ccrow.at[0:COARSE])]),
                      send(-1, [(ccrow.at[COARSE:2 * COARSE], ccrow.at[2 * COARSE:3 * COARSE])])]
 
@@ -216,8 +270,8 @@
 
     for c in range(4):
         dg[2 * c:2 * c + 2] = rhs_ref[:, c * LANES:(c + 1) * LANES].T.reshape(2, 8, 8, LANES)
-    own_ghosts(coef, True)
-    far_ghosts(0, coef, coef_handles)
+    own_ghosts(coef, ghost, keep_own=True)
+    far_ghosts(recv.at[0], coef, ghost, coef_handles)
 
     def weigh(x, g, w, lives, finish):
         mask4 = jnp.where((row == 0) & (lives[4] == 0), 0.0, 1.0)[None]
@@ -249,12 +303,26 @@
     def fine_finish(i, diag, inverse):
         bd[i] = dg[i] * inverse
         dg[i] = diag
+        xb[9, i + 1, 1:9] = inverse
 
     weigh(coef, ghost, wt, [fmask[6 + f] for f in range(6)], fine_finish)
 
-    own_ghosts(x0, False)
-    far_ghosts(1, x0, x0_handles)
+    inverse_handles = start_faces(3, xb.at[9])
+    own_ghosts(x0, ghost)
+    far_ghosts(recv.at[1], x0, ghost, x0_handles)
     sweep(x0, ghost, wt, bd, upd, xb.at[2], 0)
+    for handle in link_handles:
+        arrived(handle)
+    for side in range(2):
+        for k in range(3):
+            f = 2 * k + side
+            cut = (0 if side == 0 else 7,)
+            cut = (slice(None),) * k + cut
+            wface[f] = wt[(f,) + cut] * dg[cut]
+            ids = jnp.broadcast_to(nlinks[side, 2 * k + 1 - side:2 * k + 2 - side], (8, LANES))
+            nidx[side, k] = jnp.bitwise_and(ids, FINE - 1)
+            linked = (ids >= 0) & (jnp.right_shift(ids, 7) == me) & valid[1 if side else -1]
+            nmask[side, k] = jnp.where(linked, 1, 0)
 
     own_lane = (jnp.right_shift(lane, 5) == 1)
     group = jnp.right_shift(lane, 5)
@@ -328,11 +396,17 @@
             block = idrow[:, c * LANES:(c + 1) * LANES].T
             cidg[2 * c:2 * c + 2] = block.reshape(2, 8, 8, LANES)
 
-    exchange(2, xb.at[2], coarse_setup_a)
-    sweep(xb.at[2], ghost, wt, bd, upd, xb.at[3], 1)
-    exchange(3, xb.at[3], coarse_setup_b)
-    sweep(xb.at[3], ghost, wt, bd, upd, xb.at[4], 2)
-    exchange(4, xb.at[4], coarse_setup_c)
+    def setup_first():
+        for handle in inverse_handles:
+            arrived(handle)
+        coarse_setup_a()
+        coarse_setup_b()
+
+    two_sweeps(xb.at[2], ghost, xb.at[3], ghost3, xb.at[4], xb.at[10], 6, setup_first)
+    x3_handles = start_faces(4, xb.at[4])
+    own_ghosts(xb.at[4], ghost)
+    coarse_setup_c()
+    far_ghosts(recv.at[4], xb.at[4], ghost, x3_handles)
 
     x3 = xb.at[4]
 
@@ -413,17 +487,26 @@
                 at = 16 * i + 8 * half
                 back[k, at:at + 8] = jnp.where(row < 4, quads[2 * half], quads[2 * half + 1])
         if k == 1:
-            b_handles = [send(1, [(back.at[1], backr.at[0])]), send(-1, [(back.at[1], backr.at[1])])]
+            b_handles = [send(1, [(back.at[1], backr.at[0])]), send(-1, [(back.at[1], backr.at[1])]),
+                         send(2, [(back.at[1], backr.at[2])]), send(-2, [(back.at[1], backr.at[3])])]
+        else:
+            b_handles += [send(1, [(back.at[0], backr.at[4])]), send(-1, [(back.at[0], backr.at[5])])]
     for c in range(4):
         block = c3[2 * c + 1:2 * c + 3, 1:9].reshape(LANES, LANES).T
         cout_ref[:, c * LANES:(c + 1) * LANES] = block[COARSE:2 * COARSE]
     for handle in b_handles:
         arrived(handle)
-    from_prev = jnp.where(lane < counts[2, 0], 1, 0)
-    from_next = jnp.where(lane >= FINE - counts[2, 1], 1, 0)
-    from_prev = jnp.broadcast_to(from_prev[None], (8, 8, LANES)).reshape(64, LANES)
-    from_next = jnp.broadcast_to(from_next[None], (8, 8, LANES)).reshape(64, LANES)
-    values = jnp.where(from_prev != 0, backr[0], jnp.where(from_next != 0, backr[1], back[0]))
+
+    def by_owner(at, before, here, after):
+        low = jnp.where(lane < known(at, 0), 1, 0)
+        high = jnp.where(lane >= FINE - known(at, 1), 1, 0)
+        low = jnp.broadcast_to(low[None], (8, 8, LANES)).reshape(64, LANES)
+        high = jnp.broadcast_to(high[None], (8, 8, LANES)).reshape(64, LANES)
+        return jnp.where(low != 0, before, jnp.where(high != 0, after, here))
+
+    values = by_owner(2, backr[0], back[0], backr[1])
+    near[0] = by_owner(1, backr[2], backr[4], back[1])
+    near[1] = by_owner(3, back[1], backr[5], backr[3])
     expand[pl.ds(0, 64, stride=2)] = values
     expand[pl.ds(1, 64, stride=2)] = values
 
@@ -434,9 +517,25 @@
 
     lax.fori_loop(0, 8, correct_step, 0, unroll=True)
 
-    for at in range(3):
-        exchange(5 + at, xb.at[5 + at])
-        sweep(xb.at[5 + at], ghost, wt, bd, upd, xb.at[6 + at], at)
+    for f in range(6):
+        k, side = f // 2, f % 2
+        edge = 0 if side else 3
+        if k == 0:
+            part = near[side, 16 * edge:16 * edge + 16]
+        elif k == 1:
+            part = jnp.concatenate([near[side, 16 * i + 4 * edge:16 * i + 4 * edge + 4] for i in range(4)], axis=0)
+        else:
+            part = near[side, pl.ds(edge, 16, stride=4)]
+        part = pick(part, fidx[f])
+        expand2[f, pl.ds(0, 16, stride=2)] = part
+        expand2[f, pl.ds(1, 16, stride=2)] = part
+        four = expand2[f].reshape(4, 1, 8, LANES)
+        far = get_ghost(x3, ghost, f) + jnp.broadcast_to(four, (4, 2, 8, LANES)).reshape(8, 8, LANES)
+        own = pick_face(face(xb.at[5], f ^ 1), fidx[f])
+        put_ghost(xb.at[5], ghost2, f, jnp.where(fmask[f][None] != 0, far, own))
+
+    sweep(xb.at[5], ghost2, wt, bd, upd, xb.at[6], 0)
+    two_sweeps(xb.at[6], ghost, xb.at[7], ghost3, xb.at[8], xb.at[11], 8)
     for c in range(4):
         block = xb[8, 2 * c + 1:2 * c + 3, 1:9].reshape(LANES, LANES).T
         out_ref[:, c * LANES:(c + 1) * LANES] = block
@@ -469,14 +568,14 @@
                 pltpu.VMEM((6, FINE), i32),
                 pltpu.VMEM((1, FINE), i32),
                 pltpu.VMEM((6, COARSE), i32),
-                pltpu.VMEM((9,) + padded, f32),
+                pltpu.VMEM((12,) + padded, f32),
                 pltpu.VMEM((6,) + volume, f32),
                 pltpu.VMEM(volume, f32),
                 pltpu.VMEM(volume, f32),
                 pltpu.VMEM(volume, f32),
                 pltpu.VMEM((2, 8, 8, LANES), f32),
-                pltpu.VMEM((8, 2, 8, 8, LANES), f32),
-                pltpu.VMEM((8, 2, 3, 8, 8, LANES), f32),
+                pltpu.VMEM((10, 2, 8, 8, LANES), f32),
+                pltpu.VMEM((10, 2, 3, 8, 8, LANES), f32),
                 pltpu.VMEM((6, 8, LANES), i32),
                 pltpu.VMEM((12, 8, LANES), i32),
                 pltpu.VMEM((LANES, 512), f32),
@@ -499,8 +598,20 @@
                 pltpu.VMEM((2, 32, LANES), f32),
                 pltpu.VMEM((LANES, LANES), f32),
                 pltpu.VMEM((2, 64, LANES), f32),
+                pltpu.VMEM((6, 64, LANES), f32),
+                pltpu.VMEM((LANES, LANES), f32),
                 pltpu.VMEM((2, 64, LANES), f32),
-                pltpu.VMEM((LANES, LANES), f32),
+                pltpu.VMEM((6, 32, LANES), f32),
+                pltpu.VMEM((2, 8, 8, LANES), f32),
+                pltpu.VMEM((2, 6, FINE), i32),
+                pltpu.VMEM((2, 3, 8, LANES), i32),
+                pltpu.VMEM((2, 3, 8, LANES), i32),
+                pltpu.VMEM((6, 8, 8, LANES), f32),
+                pltpu.VMEM((2, 3, 8, 8, LANES), f32),
+                pltpu.VMEM((2, 2, 6, 8, LANES), f32),
+                pltpu.VMEM((2, 2, 6, 8, LANES), f32),
+                pltpu.VMEM((2, 3, 8, 8, LANES), f32),
+                pltpu.VMEM((2, 8, 8, LANES), f32),
                 pltpu.SemaphoreType.DMA((N_COPIES,)),
                 pltpu.SemaphoreType.DMA((N_COPIES,)),
                 pltpu.SemaphoreType.DMA((7,)),

time: 65.9 us -> 52.4 us (0.80)
  Pallas kernels: 62.4 us -> 48.6 us
    pallas_call x1, Pallas kernels: 62.4 us -> 48.6 us  [on_device(): pl.pallas_call(functools.partial(kernel, gx, gy), out_shape=(jax.ShapeDty...]
where the time goes in v3:
time: 52.4 us; the launch traced here: 51.6 us
  Pallas kernels  48.6 us (93%)
  local copies, waits for them, and re-layouts  2.34 us (4%)
  between operations  0.65 us (1%)
    pallas_call x1, Pallas kernels, on_device(): pl.pallas_call(functools.partial(kernel, gx, gy), out_shape=(jax.ShapeDty...  48.6 us
    unnamed x4, local copies, waits for them, and re-layouts  2.34 us

profile of v3, /device:TPU:32, one launch (start us, length us, event | category | flops | bytes accessed | tf_op | source)
XLA Modules:
  0.0 51.6 jit_solution(8232866683228921346)
XLA Ops:
  0.6 48.6 %shard_map.86 = (f32[128,512]{1,0:T(8,128)}, f32[32,512]{1,0:T(8,128)}) custom-call(f32[128,512]{1,0:T(8,128)} %rhs_hbm.1, f32[128,512]{1,0:T(8,128)} %guess_hbm.1, f32[128,512]{1,0:T(8,128)} %coef_hbm.1, s32[6,128]{1,0:T(8,128)} %bitcast.3, s32[1,128]{1,0:T(1,128)} %bitcast.5, f32[32,512]{1,0:T(8,128)} %ccoef_hbm.1, s32[6,32]{1,0:T(8,128)} %bitcast.4), custom_call_target="tpu_custom_call" | custom-call | tf_op jit(solution)/shard_map/pallas_call | solution.py:559
  49.2 0.0 copy-start
  49.2 1.7 %copy.11 = f32[128,512]{1,0:T(8,128)} copy(f32[128,512]{1,0:T(8,128)} %get-tuple-element.4) | data formatting | bytes 524288
  50.9 0.0 copy-done
  50.9 0.6 %copy.12 = f32[32,512]{1,0:T(8,128)} copy(f32[32,512]{1,0:T(8,128)S(1)} %copy-done) | data formatting | bytes 131072
Async XLA Ops:
  49.2 1.7 %copy-start = (f32[32,512]{1,0:T(8,128)S(1)}, f32[32,512]{1,0:T(8,128)}, u32[]{:S(2)}) copy-start(f32[32,512]{1,0:T(8,128)} %get-tuple-element.5) | copy-start | bytes 196612

commit v4 on v3

--- a/solution.py
+++ b/solution.py
@@ -39,20 +39,20 @@
     rhs_ref, guess_ref, coef_ref, links_ref, owner_ref, clinks_ref,
     xb, wt, bd, dg, upd, ghost, packed, recv, fidx, fmask,
     ccrow, cxb, cwt, cidg, cbd, cupd, cghost, idrow, tidx, tsrc, cidx, crec, cpack, cnidx,
-    counts, src, pair2, pair2r, tall, back, backr, expand, near, expand2, ghost2,
-    nlinks, nidx, nmask, wface, flux, edges, erecv, beside, ghost3,
+    counts, src, pair2, pair2r, tall, back, backr, backp, backpr, expand, near, expand2, ghost2,
+    nlinks, nidx, nmask, wface, flux, edges, erecv, beside, ghost3, local, psi, psir, halved,
     ssem, rsem, isem,
 ):
     devices = gx * gy
     me = lax.axis_index("gx") * gy + lax.axis_index("gy")
-    valid = {1: me < devices - 1, -1: me > 0, 2: me < devices - 2, -2: me > 1}
+    valid = {1: me < devices - 1, -1: me > 0, 2: me < devices - 2, -2: me > 1, 3: me < devices - 3, -3: me > 2}
 
     def device(offset):
         target = lax.rem(me + offset + devices, devices)
         return (target // gy, lax.rem(target, gy))
 
     barrier = pltpu.get_barrier_semaphore()
-    for offset in (1, -1, 2, -2):
+    for offset in valid:
         @pl.when(valid[offset])
         def _():
             pl.semaphore_signal(barrier, inc=1, device_id=device(offset), device_id_type=MESH)
@@ -251,7 +251,7 @@
     counts[2, 1] = jnp.broadcast_to(to_next, (8, LANES))
     ccrow[3 * COARSE:] = jnp.ones((COARSE, 512), jnp.float32)
 
-    pl.semaphore_wait(barrier, jnp.minimum(me, 2) + jnp.minimum(devices - 1 - me, 2))
+    pl.semaphore_wait(barrier, jnp.minimum(me, 3) + jnp.minimum(devices - 1 - me, 3))
 
     coef_handles = start_faces(0, coef)
     x0_handles = start_faces(1, x0)
@@ -403,12 +403,42 @@
         coarse_setup_b()
 
     two_sweeps(xb.at[2], ghost, xb.at[3], ghost3, xb.at[4], xb.at[10], 6, setup_first)
-    x3_handles = start_faces(4, xb.at[4])
-    own_ghosts(xb.at[4], ghost)
-    coarse_setup_c()
-    far_ghosts(recv.at[4], xb.at[4], ghost, x3_handles)
-
     x3 = xb.at[4]
+    psi[...] = jnp.zeros((2, 64, LANES), jnp.float32)
+    for side in range(2):
+        edge = 0 if side else 3
+        for k in range(3):
+            f = 2 * k + side
+            pairs = (face(x3, f) * wface[f]).reshape(4, 2, 8, LANES)
+            pairs = pairs[:, 0] + pairs[:, 1]
+            pairs = 0.5 * (pairs + pltpu.roll(pairs, 7, 1))
+            halved[f] = pairs.reshape(32, LANES)
+            part = pick(halved[f, pl.ds(0, 16, stride=2)], nidx[side, k])
+            mask = jnp.broadcast_to(nmask[side, k][None], (2, 8, LANES)).reshape(16, LANES)
+            part = jnp.where(mask != 0, part, 0.0)
+            if k == 0:
+                psi[side, 16 * edge:16 * edge + 16] = part
+            elif k == 1:
+                for i in range(4):
+                    at = 16 * i + 4 * edge
+                    psi[side, at:at + 4] = psi[side, at:at + 4] + part[4 * i:4 * i + 4]
+            else:
+                psi[side, pl.ds(edge, 16, stride=4)] = psi[side, pl.ds(edge, 16, stride=4)] + part
+    low_lane = jnp.broadcast_to((lane < 64)[None], (4, 8, LANES)).reshape(32, LANES)
+
+    def pack(values, keep_low):
+        turned = pltpu.roll(values[32:], 64, 1)
+        return jnp.where(low_lane, values[:32], turned) if keep_low else jnp.where(low_lane, turned, values[:32])
+
+    for at, (side, distance) in enumerate(((0, 1), (1, -1), (1, 3), (0, -3))):
+        pair2[2 + at] = pack(psi[side], distance < 0)
+    r_handles = [send(3, [(pair2.at[4], pair2r.at[4])]), send(-3, [(pair2.at[5], pair2r.at[5])]),
+                 send(2, [(psi.at[1], psir.at[2])]), send(-2, [(psi.at[0], psir.at[3])]),
+                 send(1, [(psi.at[1], psir.at[0]), (pair2.at[2], pair2r.at[2])]),
+                 send(-1, [(psi.at[0], psir.at[1]), (pair2.at[3], pair2r.at[3])])]
+
+    own_ghosts(xb.at[4], ghost, zero_far=True)
+
 
     def restrict_step(i, carry):
         total = jnp.zeros((4, 8, LANES), jnp.float32)
@@ -422,17 +452,22 @@
 
     lax.fori_loop(0, 4, restrict_step, 0, unroll=True)
     restricted = tall[pl.ds(0, 64, stride=2)]
-    src[2] = restricted
-    low_lane = jnp.broadcast_to((lane < 64)[None], (4, 8, LANES)).reshape(32, LANES)
-    turned = pltpu.roll(restricted[32:], 64, 1)
-    pair2[0] = jnp.where(low_lane, turned, restricted[:32])
-    pair2[1] = jnp.where(low_lane, restricted[:32], turned)
-    r_handles = [send(1, [(src.at[2], src.at[1])]), send(-1, [(src.at[2], src.at[3])]),
-                 send(2, [(pair2.at[0], pair2r.at[0])]), send(-2, [(pair2.at[1], pair2r.at[1])])]
+    local[...] = restricted
+    pair2[0] = pack(restricted, False)
+    pair2[1] = pack(restricted, True)
+    r_handles += [send(2, [(pair2.at[0], pair2r.at[0])]), send(-2, [(pair2.at[1], pair2r.at[1])]),
+                  send(1, [(local, src.at[1])]), send(-1, [(local, src.at[3])])]
+    x3_handles = start_faces(4, x3)
+    coarse_setup_c()
     for handle in r_handles:
         arrived(handle)
-    src[0, 0:32] = jnp.where(low_lane, pair2r[1], pair2r[0])
-    src[0, 32:64] = pltpu.roll(jnp.where(low_lane, pair2r[0], pair2r[1]), 64, 1)
+    src[1] = src[1] + psi[0] + jnp.where(valid[-2], psir[2], 0.0)
+    src[3] = src[3] + psi[1] + jnp.where(valid[2], psir[3], 0.0)
+    src[2] = local[...] + jnp.where(valid[-1], psir[0], 0.0) + jnp.where(valid[1], psir[1], 0.0)
+    high = pair2r[0] + pair2r[2] + jnp.where(valid[-3], pair2r[4], 0.0)
+    low = pair2r[1] + pair2r[3] + jnp.where(valid[3], pair2r[5], 0.0)
+    src[0, 0:32] = jnp.where(low_lane, low, high)
+    src[0, 32:64] = pltpu.roll(jnp.where(low_lane, high, low), 64, 1)
 
     for o in range(4):
         ox, oy = o // 2, o % 2
@@ -464,8 +499,10 @@
     c_handles = [send(1, [(cpack.at[1], crec.at[0])]), send(-1, [(cpack.at[0], crec.at[1])])]
     for f in range(6):
         put_ghost(c2, cghost, f, pick_face(face(c2, f ^ 1), cidx[f]))
+    far_ghosts(recv.at[4], x3, ghost, x3_handles)
     for side in range(2):
         arrived(c_handles[side])
+    for side in range(2):
         for k in range(3):
             f = 2 * k + side
             value = pick(crec[side], cnidx[f]).reshape(8, 8, LANES)
@@ -487,10 +524,12 @@
                 at = 16 * i + 8 * half
                 back[k, at:at + 8] = jnp.where(row < 4, quads[2 * half], quads[2 * half + 1])
         if k == 1:
-            b_handles = [send(1, [(back.at[1], backr.at[0])]), send(-1, [(back.at[1], backr.at[1])]),
-                         send(2, [(back.at[1], backr.at[2])]), send(-2, [(back.at[1], backr.at[3])])]
+            backp[0] = pack(back[1], True)
+            backp[1] = pack(back[1], False)
+            b_handles = [send(2, [(backp.at[0], backpr.at[2])]), send(-2, [(backp.at[1], backpr.at[3])]),
+                         send(1, [(backp.at[0], backpr.at[0])]), send(-1, [(backp.at[1], backpr.at[1])])]
         else:
-            b_handles += [send(1, [(back.at[0], backr.at[4])]), send(-1, [(back.at[0], backr.at[5])])]
+            b_handles += [send(1, [(back.at[0], backr.at[0])]), send(-1, [(back.at[0], backr.at[1])])]
     for c in range(4):
         block = c3[2 * c + 1:2 * c + 3, 1:9].reshape(LANES, LANES).T
         cout_ref[:, c * LANES:(c + 1) * LANES] = block[COARSE:2 * COARSE]
@@ -504,9 +543,12 @@
         high = jnp.broadcast_to(high[None], (8, 8, LANES)).reshape(64, LANES)
         return jnp.where(low != 0, before, jnp.where(high != 0, after, here))
 
-    values = by_owner(2, backr[0], back[0], backr[1])
-    near[0] = by_owner(1, backr[2], backr[4], back[1])
-    near[1] = by_owner(3, back[1], backr[5], backr[3])
+    first_half, last_half = [
+        jnp.concatenate([backpr[at], pltpu.roll(backpr[at], 64, 1)], axis=0) for at in (0, 2)], [
+        jnp.concatenate([backpr[at], pltpu.roll(backpr[at], 64, 1)], axis=0) for at in (1, 3)]
+    values = by_owner(2, first_half[0], back[0], last_half[0])
+    near[0] = by_owner(1, first_half[1], backr[0], back[1])
+    near[1] = by_owner(3, back[1], backr[1], last_half[1])
     expand[pl.ds(0, 64, stride=2)] = values
     expand[pl.ds(1, 64, stride=2)] = values
 
@@ -540,7 +582,7 @@
         block = xb[8, 2 * c + 1:2 * c + 3, 1:9].reshape(LANES, LANES).T
         out_ref[:, c * LANES:(c + 1) * LANES] = block
 
-    for offset in (1, -1, 2, -2):
+    for offset in valid:
         @pl.when(valid[offset])
         def _():
             for o, made in sent:
@@ -549,6 +591,20 @@
                         copy.wait_send()
 
 
+def deliver(fine_ref, coarse_ref, fine_out, coarse_out, fine, coarse, in_sem, out_sem):
+    parts = [(fine_ref.at[32 * c:32 * c + 32], fine.at[32 * c:32 * c + 32], fine_out.at[32 * c:32 * c + 32]) for c in range(4)]
+    parts.append((coarse_ref, coarse, coarse_out))
+    fetches = [pltpu.make_async_copy(source, middle, in_sem.at[at]) for at, (source, middle, _) in enumerate(parts)]
+    stores = [pltpu.make_async_copy(middle, target, out_sem.at[at]) for at, (_, middle, target) in enumerate(parts)]
+    for fetch in fetches:
+        fetch.start()
+    for fetch, store in zip(fetches, stores):
+        fetch.wait()
+        store.start()
+    for store in stores:
+        store.wait()
+
+
 def solution(mesh):
     gx, gy = mesh.shape["gx"], mesh.shape["gy"]
     f32, i32 = jnp.float32, jnp.int32
@@ -556,7 +612,7 @@
     def on_device(rhs, guess, coef, links, owner, ccoef, clinks):
         whole = pl.BlockSpec(memory_space=pltpu.VMEM)
         volume, padded = (8, 8, 8, LANES), (10, 10, 8, LANES)
-        return pl.pallas_call(
+        results = pl.pallas_call(
             functools.partial(kernel, gx, gy),
             out_shape=(jax.ShapeDtypeStruct((FINE, 512), f32), jax.ShapeDtypeStruct((COARSE, 512), f32)),
             in_specs=[pl.BlockSpec(memory_space=pltpu.HBM)] * 7,
@@ -594,11 +650,13 @@
                 pltpu.VMEM((12, 8, LANES), i32),
                 pltpu.VMEM((5, 2, 8, LANES), i32),
                 pltpu.VMEM((4, 64, LANES), f32),
-                pltpu.VMEM((2, 32, LANES), f32),
-                pltpu.VMEM((2, 32, LANES), f32),
+                pltpu.VMEM((6, 32, LANES), f32),
+                pltpu.VMEM((6, 32, LANES), f32),
                 pltpu.VMEM((LANES, LANES), f32),
                 pltpu.VMEM((2, 64, LANES), f32),
-                pltpu.VMEM((6, 64, LANES), f32),
+                pltpu.VMEM((2, 64, LANES), f32),
+                pltpu.VMEM((2, 32, LANES), f32),
+                pltpu.VMEM((4, 32, LANES), f32),
                 pltpu.VMEM((LANES, LANES), f32),
                 pltpu.VMEM((2, 64, LANES), f32),
                 pltpu.VMEM((6, 32, LANES), f32),
@@ -612,12 +670,25 @@
                 pltpu.VMEM((2, 2, 6, 8, LANES), f32),
                 pltpu.VMEM((2, 3, 8, 8, LANES), f32),
                 pltpu.VMEM((2, 8, 8, LANES), f32),
+                pltpu.VMEM((64, LANES), f32),
+                pltpu.VMEM((2, 64, LANES), f32),
+                pltpu.VMEM((4, 64, LANES), f32),
+                pltpu.VMEM((6, 32, LANES), f32),
                 pltpu.SemaphoreType.DMA((N_COPIES,)),
                 pltpu.SemaphoreType.DMA((N_COPIES,)),
                 pltpu.SemaphoreType.DMA((7,)),
             ],
             compiler_params=pltpu.CompilerParams(collective_id=0, has_side_effects=True, vmem_limit_bytes=56 * 1024 * 1024),
         )(rhs, guess, coef, links.T, owner.T, ccoef, clinks.T)
+        hbm = pl.BlockSpec(memory_space=pltpu.HBM)
+        return pl.pallas_call(
+            deliver,
+            out_shape=(jax.ShapeDtypeStruct((FINE, 512), f32), jax.ShapeDtypeStruct((COARSE, 512), f32)),
+            in_specs=[hbm, hbm],
+            out_specs=(hbm, hbm),
+            scratch_shapes=[pltpu.VMEM((FINE, 512), f32), pltpu.VMEM((COARSE, 512), f32),
+                            pltpu.SemaphoreType.DMA((5,)), pltpu.SemaphoreType.DMA((5,))],
+        )(*results)
 
     rows = P(("gx", "gy"), None)
     return jax.shard_map(on_device, mesh=mesh, in_specs=(rows,) * 7, out_specs=(rows, rows), check_vma=False)

time: 52.4 us -> 48.8 us (0.931)
  local copies, waits for them, and re-layouts: 2.34 us -> 0 us
  Pallas kernels: 48.6 us -> 47.7 us
    pallas_call x1, Pallas kernels: 48.6 us -> 46 us  [on_device(): pl.pallas_call(functools.partial(kernel, gx, gy), out_shape=(jax.ShapeDty...]
    unnamed x4 -> x0, local copies, waits for them, and re-layouts: 2.34 us -> none
    pallas_call x0 -> x1, Pallas kernels: none -> 1.68 us  [on_device(): pl.pallas_call(deliver, out_shape=(jax.ShapeDtypeStruct((FINE, 512), f32)...]
where the time goes in v4:
time: 48.8 us; the launch traced here: 48.4 us
  Pallas kernels  47.7 us (98%)
  between operations  0.64 us (1%)
    pallas_call x1, Pallas kernels, on_device(): pl.pallas_call(functools.partial(kernel, gx, gy), out_shape=(jax.ShapeDty...  46 us
    pallas_call x1, Pallas kernels, on_device(): pl.pallas_call(deliver, out_shape=(jax.ShapeDtypeStruct((FINE, 512), f32)...  1.68 us

profile of v4, /device:TPU:32, one launch (start us, length us, event | category | flops | bytes accessed | tf_op | source)
XLA Modules:
  0.0 48.4 jit_solution(8573797785543480303)
XLA Ops:
  0.6 46.0 %shard_map.86 = (f32[128,512]{1,0:T(8,128)}, f32[32,512]{1,0:T(8,128)}) custom-call(f32[128,512]{1,0:T(8,128)} %rhs_hbm.1, f32[128,512]{1,0:T(8,128)} %guess_hbm.1, f32[128,512]{1,0:T(8,128)} %coef_hbm.1, s32[6,128]{1,0:T(8,128)} %bitcast.3, s32[1,128]{1,0:T(1,128)} %bitcast.5, f32[32,512]{1,0:T(8,128)} %ccoef_hbm.1, s32[6,32]{1,0:T(8,128)} %bitcast.4), custom_call_target="tpu_custom_call" | custom-call | tf_op jit(solution)/shard_map/pallas_call | solution.py:615
  46.7 1.7 %shard_map.87 = (f32[128,512]{1,0:T(8,128)}, f32[32,512]{1,0:T(8,128)}) custom-call(f32[128,512]{1,0:T(8,128)} %get-tuple-element.4.fine_ref, f32[32,512]{1,0:T(8,128)} %get-tuple-element.5.coarse_ref), custom_call_target="tpu_custom_call" | custom-call | tf_op jit(solution)/shard_map/pallas_call | solution.py:684

commit v5 on v4

--- a/solution.py
+++ b/solution.py
@@ -19,7 +19,7 @@
 FINE = 128
 COARSE = 32
 MESH = pl.DeviceIdType.MESH
-N_COPIES = 96
+N_COPIES = 104
 
 
 def pick(values, index):
@@ -38,21 +38,22 @@
     out_ref, cout_ref,
     rhs_ref, guess_ref, coef_ref, links_ref, owner_ref, clinks_ref,
     xb, wt, bd, dg, upd, ghost, packed, recv, fidx, fmask,
-    ccrow, cxb, cwt, cidg, cbd, cupd, cghost, idrow, tidx, tsrc, cidx, crec, cpack, cnidx,
+    ccrow, cxb, cwt, cidg, cbd, cupd, cghost, idrow, tidx, tsrc, cidx, clb, ccrow2, idrow2, cidg2,
     counts, src, pair2, pair2r, tall, back, backr, backp, backpr, expand, near, expand2, ghost2,
-    nlinks, nidx, nmask, wface, flux, edges, erecv, beside, ghost3, local, psi, psir, halved,
+    nlinks, nidx, nmask, wface, flux, edges, erecv, beside, ghost3, local, psi, psir, halved, eb, ebr, eh, ehr,
     ssem, rsem, isem,
 ):
     devices = gx * gy
     me = lax.axis_index("gx") * gy + lax.axis_index("gy")
-    valid = {1: me < devices - 1, -1: me > 0, 2: me < devices - 2, -2: me > 1, 3: me < devices - 3, -3: me > 2}
+    valid = {1: me < devices - 1, -1: me > 0, 2: me < devices - 2, -2: me > 1, 3: me < devices - 3, -3: me > 2,
+             4: me < devices - 4, -4: me > 3}
 
     def device(offset):
         target = lax.rem(me + offset + devices, devices)
         return (target // gy, lax.rem(target, gy))
 
     barrier = pltpu.get_barrier_semaphore()
-    for offset in valid:
+    for offset in (1, -1):
         @pl.when(valid[offset])
         def _():
             pl.semaphore_signal(barrier, inc=1, device_id=device(offset), device_id_type=MESH)
@@ -84,13 +85,14 @@
         sent.append((offset, made))
         return (offset, made)
 
-    def arrived(handle, which=None):
-        offset, made = handle
-
-        @pl.when(valid[-offset])
-        def _():
-            for copy in (made if which is None else [made[which]]):
-                copy.wait_recv()
+    def arrived(handles):
+        for offset in valid:
+            made = [copy for to, copies in handles if to == offset for copy in copies]
+            if made:
+                @pl.when(valid[-offset])
+                def _():
+                    for copy in made:
+                        copy.wait_recv()
 
     lane = lax.broadcasted_iota(jnp.int32, (8, LANES), 1)
     row = lax.broadcasted_iota(jnp.int32, (8, LANES), 0)
@@ -172,8 +174,7 @@
             put_ghost(x, g, f, value)
 
     def far_ghosts(faces, x, g, handles=()):
-        for handle in handles:
-            arrived(handle)
+        arrived(handles)
         for k in range(3):
             for side in range(2):
                 f = 2 * k + side
@@ -218,8 +219,7 @@
         far_ghosts(recv.at[e], x, g, handles)
         sweep(x, g, wt, bd, upd, middle, 1)
         own_ghosts(middle, g_middle)
-        for handle in edge_handles + list(partial_handles):
-            arrived(handle)
+        arrived(edge_handles + list(partial_handles))
         for side in range(2):
             end = 0 if side else 7
             at = 0
@@ -247,16 +247,16 @@
     owner = owner_ref[...]
     to_prev = jnp.sum((owner == me - 1).astype(jnp.float32), axis=1, keepdims=True).astype(jnp.int32)
     to_next = jnp.sum((owner == me + 1).astype(jnp.float32), axis=1, keepdims=True).astype(jnp.int32)
-    counts[2, 0] = jnp.broadcast_to(to_prev, (8, LANES))
-    counts[2, 1] = jnp.broadcast_to(to_next, (8, LANES))
-    ccrow[3 * COARSE:] = jnp.ones((COARSE, 512), jnp.float32)
-
-    pl.semaphore_wait(barrier, jnp.minimum(me, 3) + jnp.minimum(devices - 1 - me, 3))
+    counts[3, 0] = jnp.broadcast_to(to_prev, (8, LANES))
+    counts[3, 1] = jnp.broadcast_to(to_next, (8, LANES))
+
+    pl.semaphore_wait(barrier, jnp.minimum(me, 1) + jnp.minimum(devices - 1 - me, 1))
 
     coef_handles = start_faces(0, coef)
     x0_handles = start_faces(1, x0)
-    count_handles = [send(o, [(counts.at[2], counts.at[2 - o])]) for o in (1, -1, 2, -2)]
-    link_handles = [send(1, [(links_ref, nlinks.at[0])]), send(-1, [(links_ref, nlinks.at[1])])]
+    count_handles = [send(o, [(counts.at[3], counts.at[3 - o])]) for o in (1, -1)]
+    link_handles = [send(1, [(links_ref, nlinks.at[0]), (clinks_ref, clb.at[0])]),
+                    send(-1, [(links_ref, nlinks.at[1]), (clinks_ref, clb.at[1])])]
     ccoef_handles = [send(1, [(ccrow.at[COARSE:2 * COARSE], ccrow.at[0:COARSE])]),
                      send(-1, [(ccrow.at[COARSE:2 * COARSE], ccrow.at[2 * COARSE:3 * COARSE])])]
 
@@ -308,11 +308,14 @@
     weigh(coef, ghost, wt, [fmask[6 + f] for f in range(6)], fine_finish)
 
     inverse_handles = start_faces(3, xb.at[9])
+    arrived(count_handles)
+    count_handles = [send(2, [(counts.at[2:4], counts.at[0:2])]), send(-2, [(counts.at[3:5], counts.at[5:7])])]
+    ccoef_handles += [send(2, [(ccrow.at[COARSE:2 * COARSE], ccrow.at[3 * COARSE:])]),
+                      send(-2, [(ccrow.at[COARSE:2 * COARSE], ccrow2.at[3 * COARSE:])])]
     own_ghosts(x0, ghost)
     far_ghosts(recv.at[1], x0, ghost, x0_handles)
     sweep(x0, ghost, wt, bd, upd, xb.at[2], 0)
-    for handle in link_handles:
-        arrived(handle)
+    arrived(link_handles)
     for side in range(2):
         for k in range(3):
             f = 2 * k + side
@@ -324,17 +327,22 @@
             linked = (ids >= 0) & (jnp.right_shift(ids, 7) == me) & valid[1 if side else -1]
             nmask[side, k] = jnp.where(linked, 1, 0)
 
-    own_lane = (jnp.right_shift(lane, 5) == 1)
     group = jnp.right_shift(lane, 5)
     slot = jnp.bitwise_and(lane, COARSE - 1)
     coarse_handles = []
 
+    def coarse_ghost(x, x_after, f):
+        value = face(x, f ^ 1)
+        if f % 2 == 1 and x_after is not None:
+            value = jnp.where((group < 3)[None], value, face(x_after, f ^ 1))
+        return pick_face(value, cidx[f])
+
     def coarse_setup_a():
-        for handle in ccoef_handles + count_handles:
-            arrived(handle)
+        arrived(ccoef_handles + count_handles)
         load_cells(cxb.at[0], ccrow)
-        zeros = jnp.zeros((6, COARSE), jnp.int32)
-        links_c = jnp.concatenate([zeros, clinks_ref[...], zeros, zeros], axis=1)
+        load_cells(cxb.at[4], ccrow2)
+        links_c = jnp.concatenate([jnp.where(valid[-1], clb[0], -1), clinks_ref[...], jnp.where(valid[1], clb[1], -1),
+                                   jnp.full((6, COARSE), -1, jnp.int32)], axis=1)
         lives = []
         x = cxb.at[0]
         for f in range(6):
@@ -342,13 +350,9 @@
             live = ids >= 0
             step_by = jnp.right_shift(ids, 5) - me
             place = jnp.bitwise_and((step_by + 1) * COARSE + jnp.bitwise_and(ids, COARSE - 1), LANES - 1)
-            place = jnp.where(own_lane & live, place, lane)
-            cidx[f] = place
-            cnidx[f] = jnp.bitwise_and(ids, COARSE - 1) + (f // 2) * COARSE
-            cnidx[6 + f] = jnp.where(own_lane & live & (step_by != 0), 1, 0)
+            cidx[f] = jnp.where(live, place, lane)
             lives.append(jnp.where(live, 1, 0))
-            value = jnp.where(live[None], pick_face(face(x, f ^ 1), place), face(x, f))
-            put_ghost(x, cghost, f, value)
+            put_ghost(x, cghost, f, jnp.where(live[None], coarse_ghost(x, cxb.at[4], f), face(x, f)))
 
         def finish(i, diag, inverse):
             cidg[i] = inverse
@@ -357,48 +361,49 @@
         for c in range(4):
             block = cidg[2 * c:2 * c + 2].reshape(LANES, LANES).T
             idrow[COARSE:2 * COARSE, c * LANES:(c + 1) * LANES] = block[COARSE:2 * COARSE]
-        coarse_handles.append(send(1, [(idrow.at[COARSE:2 * COARSE], idrow.at[0:COARSE])]))
-        coarse_handles.append(send(-1, [(idrow.at[COARSE:2 * COARSE], idrow.at[2 * COARSE:3 * COARSE])]))
+        coarse_handles.append(send(2, [(idrow.at[COARSE:2 * COARSE], idrow.at[3 * COARSE:])]))
+        coarse_handles.append(send(-2, [(idrow.at[COARSE:2 * COARSE], idrow2.at[3 * COARSE:])]))
 
     def known(k, which):
-        return counts[k, which] if k == 2 else jnp.where(valid[k - 2], counts[k, which], 0)
+        return counts[k, which] if k == 3 else jnp.where(valid[k - 3], counts[k, which], 0)
 
     def by_group(values):
-        return jnp.where(group == 0, values[0], jnp.where(group == 1, values[1], values[2]))
+        return jnp.where(group == 0, values[0], jnp.where(group == 1, values[1], jnp.where(group == 2, values[2], values[3])))
 
     def coarse_setup_b():
-        a = [known(k, 0) for k in range(5)]
-        n = [known(k, 1) for k in range(5)]
-        stay = [FINE - a[k] - n[k] if k == 2 else jnp.where(valid[k - 2], FINE - a[k] - n[k], 0) for k in range(5)]
-        before, here = by_group(n[0:3]), by_group(stay[1:4])
-        start, after = by_group(a[1:4]), by_group(a[2:5])
-        for o in range(4):
-            rank = 8 * slot + 2 * o + jnp.where(row >= 4, 1, 0)
-            in_before = rank < before
-            in_here = rank < before + here
-            in_after = rank < before + here + after
-            at = jnp.where(in_before, FINE - before + rank, jnp.where(in_here, start + rank - before, rank - before - here))
-            step_by = jnp.where(in_before, group - 2, jnp.where(in_here, group - 1, group))
-            source = jnp.where((step_by == 2) | (step_by == -2), 0, step_by + 2)
-            tidx[o] = jnp.bitwise_and(at, LANES - 1)
-            tsrc[o] = jnp.where(in_after & (group < 3), source, 4)
-        rank_own = n[1] + lane - a[2]
-        rank_far = jnp.where(lane < 64, n[1] + stay[2] + lane, lane - FINE + n[1])
+        a = [known(k, 0) for k in range(7)]
+        n = [known(k, 1) for k in range(7)]
+        stay = [FINE - a[k] - n[k] if k == 3 else jnp.where(valid[k - 3], FINE - a[k] - n[k], 0) for k in range(7)]
+        for base, last in ((0, 1), (4, 5)):
+            before, here = by_group(n[1:4] + [n[last - 1]]), by_group(stay[2:5] + [stay[last]])
+            start, after = by_group(a[2:5] + [a[last]]), by_group(a[3:6] + [a[last + 1]])
+            place = jnp.where(group < 3, group - 1, last - 3)
+            for o in range(4):
+                rank = 8 * slot + 2 * o + jnp.where(row >= 4, 1, 0)
+                in_before = rank < before
+                in_here = rank < before + here
+                in_after = rank < before + here + after
+                at = jnp.where(in_before, FINE - before + rank, jnp.where(in_here, start + rank - before, rank - before - here))
+                step_by = jnp.where(in_before, place - 1, jnp.where(in_here, place, place + 1))
+                source = jnp.where((step_by == 3) | (step_by == -3), 5, step_by + 2)
+                tidx[2 * base + o] = jnp.bitwise_and(at, LANES - 1)
+                tsrc[base + o] = jnp.where(in_after, source, 6)
+        rank_own = n[2] + lane - a[3]
+        rank_far = jnp.where(lane < 64, n[2] + stay[3] + lane, lane - FINE + n[2])
         for k, rank in enumerate((rank_own, rank_far)):
             rank = jnp.bitwise_and(rank, 255)
             tidx[4 + 2 * k] = COARSE + jnp.right_shift(rank, 3)
             tidx[5 + 2 * k] = jnp.bitwise_and(rank, 7)
 
     def coarse_setup_c():
-        for handle in coarse_handles:
-            arrived(handle)
+        arrived(coarse_handles)
         for c in range(4):
-            block = idrow[:, c * LANES:(c + 1) * LANES].T
-            cidg[2 * c:2 * c + 2] = block.reshape(2, 8, 8, LANES)
+            block = idrow[:, c * LANES:(c + 1) * LANES].T.reshape(2, 8, 8, LANES)
+            cidg[2 * c:2 * c + 2] = jnp.where((group < 3)[None, None], cidg[2 * c:2 * c + 2], block)
+            cidg2[2 * c:2 * c + 2] = idrow2[:, c * LANES:(c + 1) * LANES].T.reshape(2, 8, 8, LANES)
 
     def setup_first():
-        for handle in inverse_handles:
-            arrived(handle)
+        arrived(inverse_handles)
         coarse_setup_a()
         coarse_setup_b()
 
@@ -430,12 +435,32 @@
         turned = pltpu.roll(values[32:], 64, 1)
         return jnp.where(low_lane, values[:32], turned) if keep_low else jnp.where(low_lane, turned, values[:32])
 
+    def pack_edges(values, keep_low):
+        turned = pltpu.roll(values[8:], 64, 1)
+        return jnp.where(lane < 64, values[:8], turned) if keep_low else jnp.where(lane < 64, turned, values[:8])
+
+    def edge_places(upper):
+        return (slice(60, 64), pl.ds(51, 4, stride=4), pl.ds(15, 4, stride=16)) if upper else (
+            slice(0, 4), pl.ds(0, 4, stride=4), pl.ds(0, 4, stride=16))
+
+    def edge_rows(ref, upper):
+        parts = [ref[place] for place in edge_places(upper)]
+        return jnp.concatenate(parts + parts[:1], axis=0)
+
     for at, (side, distance) in enumerate(((0, 1), (1, -1), (1, 3), (0, -3))):
         pair2[2 + at] = pack(psi[side], distance < 0)
-    r_handles = [send(3, [(pair2.at[4], pair2r.at[4])]), send(-3, [(pair2.at[5], pair2r.at[5])]),
-                 send(2, [(psi.at[1], psir.at[2])]), send(-2, [(psi.at[0], psir.at[3])]),
-                 send(1, [(psi.at[1], psir.at[0]), (pair2.at[2], pair2r.at[2])]),
-                 send(-1, [(psi.at[0], psir.at[1]), (pair2.at[3], pair2r.at[3])])]
+    for ahead in (1, 0):
+        base = 0 if ahead else 3
+        back_edges, ahead_edges = edge_rows(psi.at[1 - ahead], ahead), edge_rows(psi.at[ahead], ahead)
+        eb[base], eb[base + 2] = back_edges, ahead_edges
+        eh[base], eh[base + 2] = pack_edges(back_edges, not ahead), pack_edges(ahead_edges, not ahead)
+    r_handles = [send(4, [(eh.at[2], ehr.at[2])]), send(-4, [(eh.at[5], ehr.at[5])]),
+                 send(3, [(pair2.at[4], pair2r.at[4]), (eb.at[2], ebr.at[2])]),
+                 send(-3, [(pair2.at[5], pair2r.at[5]), (eb.at[5], ebr.at[5])]),
+                 send(2, [(psi.at[1], psir.at[2]), (eh.at[0], ehr.at[0])]),
+                 send(-2, [(psi.at[0], psir.at[3]), (eh.at[3], ehr.at[3])]),
+                 send(1, [(psi.at[1], psir.at[0]), (pair2.at[2], pair2r.at[2]), (eb.at[0], ebr.at[0])]),
+                 send(-1, [(psi.at[0], psir.at[1]), (pair2.at[3], pair2r.at[3]), (eb.at[3], ebr.at[3])])]
 
     own_ghosts(xb.at[4], ghost, zero_far=True)
 
@@ -455,19 +480,33 @@
     local[...] = restricted
     pair2[0] = pack(restricted, False)
     pair2[1] = pack(restricted, True)
-    r_handles += [send(2, [(pair2.at[0], pair2r.at[0])]), send(-2, [(pair2.at[1], pair2r.at[1])]),
+    for ahead in (1, 0):
+        base = 0 if ahead else 3
+        own_edges = edge_rows(local, ahead)
+        eb[base + 1] = own_edges
+        eh[base + 1] = pack_edges(own_edges, not ahead)
+    r_handles += [send(3, [(eh.at[1], ehr.at[1])]), send(-3, [(eh.at[4], ehr.at[4])]),
+                  send(2, [(pair2.at[0], pair2r.at[0]), (eb.at[1], ebr.at[1])]),
+                  send(-2, [(pair2.at[1], pair2r.at[1]), (eb.at[4], ebr.at[4])]),
                   send(1, [(local, src.at[1])]), send(-1, [(local, src.at[3])])]
     x3_handles = start_faces(4, x3)
     coarse_setup_c()
-    for handle in r_handles:
-        arrived(handle)
+    arrived(r_handles)
     src[1] = src[1] + psi[0] + jnp.where(valid[-2], psir[2], 0.0)
     src[3] = src[3] + psi[1] + jnp.where(valid[2], psir[3], 0.0)
     src[2] = local[...] + jnp.where(valid[-1], psir[0], 0.0) + jnp.where(valid[1], psir[1], 0.0)
     high = pair2r[0] + pair2r[2] + jnp.where(valid[-3], pair2r[4], 0.0)
     low = pair2r[1] + pair2r[3] + jnp.where(valid[3], pair2r[5], 0.0)
-    src[0, 0:32] = jnp.where(low_lane, low, high)
-    src[0, 32:64] = pltpu.roll(jnp.where(low_lane, high, low), 64, 1)
+    src[0] = jnp.concatenate([high, pltpu.roll(high, 64, 1)], axis=0)
+    src[4] = jnp.concatenate([low, pltpu.roll(low, 64, 1)], axis=0)
+    for ahead in (1, 0):
+        base, sign = (0, -1) if ahead else (3, 1)
+        edge_two = ebr[base] + ebr[base + 1] + jnp.where(valid[3 * sign], ebr[base + 2], 0.0)
+        edge_three = ehr[base] + ehr[base + 1] + jnp.where(valid[4 * sign], ehr[base + 2], 0.0)
+        edge_three = jnp.concatenate([edge_three, pltpu.roll(edge_three, 64, 1)], axis=0)
+        for at, place in enumerate(edge_places(ahead)):
+            src[0 if ahead else 4, place] = edge_two[4 * at:4 * at + 4]
+            src[5, place] = edge_three[4 * at:4 * at + 4]
 
     for o in range(4):
         ox, oy = o // 2, o % 2
@@ -476,7 +515,7 @@
             for j in range(4):
                 q = 4 * (4 * i + j)
                 value = jnp.zeros((8, LANES), jnp.float32)
-                for k in range(4):
+                for k in range(6):
                     four = src[k, q:q + 4]
                     taken = pick(jnp.concatenate([four, four], axis=0), index)
                     value = jnp.where(which == k, taken, value)
@@ -486,27 +525,20 @@
                 update = scaled * (1.0 / THETA)
                 cupd[at[0], at[1]] = update
                 cxb[1, at[0] + 1, at[1] + 1] = update
+                if at[0] == 0 or at[1] == 0:
+                    for k in (3, 4, 5):
+                        four = src[k, q:q + 4]
+                        taken = pick(jnp.concatenate([four, four], axis=0), tidx[8 + o])
+                        value = taken if k == 3 else jnp.where(tsrc[4 + o] == k, taken, value)
+                    value = jnp.where(tsrc[4 + o] < 6, value, 0.0)
+                    cxb[5, at[0] + 1, at[1] + 1] = value * cidg2[at[0], at[1]] * (1.0 / THETA)
 
     c1, c2, c3 = cxb.at[1], cxb.at[2], cxb.at[3]
     for f in range(6):
-        put_ghost(c1, cghost, f, pick_face(face(c1, f ^ 1), cidx[f]))
+        put_ghost(c1, cghost, f, coarse_ghost(c1, cxb.at[5], f))
     sweep(c1, cghost, cwt, cbd, cupd, c2, 1)
-
-    lane64 = jnp.broadcast_to(lane[None], (8, 8, LANES)).reshape(64, LANES)
-    for side in range(2):
-        faces = [face(c2, 2 * k + side).reshape(64, LANES) for k in range(3)]
-        cpack[side] = jnp.where(lane64 < 32, pltpu.roll(faces[0], 96, 1), jnp.where(lane64 < 64, faces[1], pltpu.roll(faces[2], 32, 1)))
-    c_handles = [send(1, [(cpack.at[1], crec.at[0])]), send(-1, [(cpack.at[0], crec.at[1])])]
     for f in range(6):
-        put_ghost(c2, cghost, f, pick_face(face(c2, f ^ 1), cidx[f]))
-    far_ghosts(recv.at[4], x3, ghost, x3_handles)
-    for side in range(2):
-        arrived(c_handles[side])
-    for side in range(2):
-        for k in range(3):
-            f = 2 * k + side
-            value = pick(crec[side], cnidx[f]).reshape(8, 8, LANES)
-            put_ghost(c2, cghost, f, jnp.where(cnidx[6 + f][None] != 0, value, get_ghost(c2, cghost, f)))
+        put_ghost(c2, cghost, f, coarse_ghost(c2, None, f))
     sweep(c2, cghost, cwt, cbd, cupd, c3, 2)
 
     for k in (1, 0):
@@ -533,8 +565,8 @@
     for c in range(4):
         block = c3[2 * c + 1:2 * c + 3, 1:9].reshape(LANES, LANES).T
         cout_ref[:, c * LANES:(c + 1) * LANES] = block[COARSE:2 * COARSE]
-    for handle in b_handles:
-        arrived(handle)
+    far_ghosts(recv.at[4], x3, ghost, x3_handles)
+    arrived(b_handles)
 
     def by_owner(at, before, here, after):
         low = jnp.where(lane < known(at, 0), 1, 0)
@@ -546,9 +578,9 @@
     first_half, last_half = [
         jnp.concatenate([backpr[at], pltpu.roll(backpr[at], 64, 1)], axis=0) for at in (0, 2)], [
         jnp.concatenate([backpr[at], pltpu.roll(backpr[at], 64, 1)], axis=0) for at in (1, 3)]
-    values = by_owner(2, first_half[0], back[0], last_half[0])
-    near[0] = by_owner(1, first_half[1], backr[0], back[1])
-    near[1] = by_owner(3, back[1], backr[1], last_half[1])
+    values = by_owner(3, first_half[0], back[0], last_half[0])
+    near[0] = by_owner(2, first_half[1], backr[0], back[1])
+    near[1] = by_owner(4, back[1], backr[1], last_half[1])
     expand[pl.ds(0, 64, stride=2)] = values
     expand[pl.ds(1, 64, stride=2)] = values
 
@@ -635,21 +667,22 @@
                 pltpu.VMEM((6, 8, LANES), i32),
                 pltpu.VMEM((12, 8, LANES), i32),
                 pltpu.VMEM((LANES, 512), f32),
-                pltpu.VMEM((4,) + padded, f32),
+                pltpu.VMEM((6,) + padded, f32),
                 pltpu.VMEM((6,) + volume, f32),
                 pltpu.VMEM(volume, f32),
                 pltpu.VMEM(volume, f32),
                 pltpu.VMEM(volume, f32),
                 pltpu.VMEM((2, 8, 8, LANES), f32),
                 pltpu.VMEM((LANES, 512), f32),
+                pltpu.VMEM((12, 8, LANES), i32),
                 pltpu.VMEM((8, 8, LANES), i32),
-                pltpu.VMEM((4, 8, LANES), i32),
                 pltpu.VMEM((6, 8, LANES), i32),
-                pltpu.VMEM((2, 64, LANES), f32),
-                pltpu.VMEM((2, 64, LANES), f32),
-                pltpu.VMEM((12, 8, LANES), i32),
-                pltpu.VMEM((5, 2, 8, LANES), i32),
-                pltpu.VMEM((4, 64, LANES), f32),
+                pltpu.VMEM((2, 6, COARSE), i32),
+                pltpu.VMEM((LANES, 512), f32),
+                pltpu.VMEM((LANES, 512), f32),
+                pltpu.VMEM(volume, f32),
+                pltpu.VMEM((7, 2, 8, LANES), i32),
+                pltpu.VMEM((6, 64, LANES), f32),
                 pltpu.VMEM((6, 32, LANES), f32),
                 pltpu.VMEM((6, 32, LANES), f32),
                 pltpu.VMEM((LANES, LANES), f32),
@@ -674,6 +707,10 @@
                 pltpu.VMEM((2, 64, LANES), f32),
                 pltpu.VMEM((4, 64, LANES), f32),
                 pltpu.VMEM((6, 32, LANES), f32),
+                pltpu.VMEM((6, 16, LANES), f32),
+                pltpu.VMEM((6, 16, LANES), f32),
+                pltpu.VMEM((6, 8, LANES), f32),
+                pltpu.VMEM((6, 8, LANES), f32),
                 pltpu.SemaphoreType.DMA((N_COPIES,)),
                 pltpu.SemaphoreType.DMA((N_COPIES,)),
                 pltpu.SemaphoreType.DMA((7,)),

time: 48.8 us -> 44.4 us (0.910)
  Pallas kernels: 47.7 us -> 43.5 us
    pallas_call x1, Pallas kernels: 46 us -> 41.9 us  [on_device(): pl.pallas_call(functools.partial(kernel, gx, gy), out_shape=(jax.ShapeDty...]
where the time goes in v5:
time: 44.4 us; the launch traced here: 44.2 us
  Pallas kernels  43.5 us (98%)
  between operations  0.64 us (1%)
    pallas_call x1, Pallas kernels, on_device(): pl.pallas_call(functools.partial(kernel, gx, gy), out_shape=(jax.ShapeDty...  41.9 us
    pallas_call x1, Pallas kernels, on_device(): pl.pallas_call(deliver, out_shape=(jax.ShapeDtypeStruct((FINE, 512), f32)...  1.68 us

profile of v5, /device:TPU:32, one launch (start us, length us, event | category | flops | bytes accessed | tf_op | source)
XLA Modules:
  0.0 44.2 jit_solution(422694366366565973)
XLA Ops:
  0.6 41.9 %shard_map.86 = (f32[128,512]{1,0:T(8,128)}, f32[32,512]{1,0:T(8,128)}) custom-call(f32[128,512]{1,0:T(8,128)} %rhs_hbm.1, f32[128,512]{1,0:T(8,128)} %guess_hbm.1, f32[128,512]{1,0:T(8,128)} %coef_hbm.1, s32[6,128]{1,0:T(8,128)} %bitcast.3, s32[1,128]{1,0:T(1,128)} %bitcast.5, f32[32,512]{1,0:T(8,128)} %ccoef_hbm.1, s32[6,32]{1,0:T(8,128)} %bitcast.4), custom_call_target="tpu_custom_call" | custom-call | tf_op jit(solution)/shard_map/pallas_call | solution.py:647
  42.5 1.7 %shard_map.87 = (f32[128,512]{1,0:T(8,128)}, f32[32,512]{1,0:T(8,128)}) custom-call(f32[128,512]{1,0:T(8,128)} %get-tuple-element.4.fine_ref, f32[32,512]{1,0:T(8,128)} %get-tuple-element.5.coarse_ref), custom_call_target="tpu_custom_call" | custom-call | tf_op jit(solution)/shard_map/pallas_call | solution.py:721

commit v6 on v5

--- a/solution.py
+++ b/solution.py
@@ -35,13 +35,14 @@
 def kernel(
     gx, gy,
     rhs_hbm, guess_hbm, coef_hbm, links_hbm, owner_hbm, ccoef_hbm, clinks_hbm,
+    out_hbm, cout_hbm,
     out_ref, cout_ref,
     rhs_ref, guess_ref, coef_ref, links_ref, owner_ref, clinks_ref,
     xb, wt, bd, dg, upd, ghost, packed, recv, fidx, fmask,
     ccrow, cxb, cwt, cidg, cbd, cupd, cghost, idrow, tidx, tsrc, cidx, clb, ccrow2, idrow2, cidg2,
     counts, src, pair2, pair2r, tall, back, backr, backp, backpr, expand, near, expand2, ghost2,
     nlinks, nidx, nmask, wface, flux, edges, erecv, beside, ghost3, local, psi, psir, halved, eb, ebr, eh, ehr,
-    ssem, rsem, isem,
+    ssem, rsem, isem, osem,
 ):
     devices = gx * gy
     me = lax.axis_index("gx") * gy + lax.axis_index("gy")
@@ -53,7 +54,7 @@
         return (target // gy, lax.rem(target, gy))
 
     barrier = pltpu.get_barrier_semaphore()
-    for offset in (1, -1):
+    for offset in (1, -1, 2, -2):
         @pl.when(valid[offset])
         def _():
             pl.semaphore_signal(barrier, inc=1, device_id=device(offset), device_id_type=MESH)
@@ -187,9 +188,8 @@
     def line(k, m, at):
         return (at,) if across(k, m) == 0 else (slice(None), at)
 
-    def two_sweeps(x, g, middle, g_middle, new, partial, e, between=None):
+    def two_sweeps(x, handles, g, middle, g_middle, new, partial, e, between=None):
         keep, gain = SWEEPS[1]
-        handles = start_faces(e, x)
         for side in range(2):
             for k in range(3):
                 f = 2 * k + side
@@ -250,7 +250,7 @@
     counts[3, 0] = jnp.broadcast_to(to_prev, (8, LANES))
     counts[3, 1] = jnp.broadcast_to(to_next, (8, LANES))
 
-    pl.semaphore_wait(barrier, jnp.minimum(me, 1) + jnp.minimum(devices - 1 - me, 1))
+    pl.semaphore_wait(barrier, jnp.minimum(me, 2) + jnp.minimum(devices - 1 - me, 2))
 
     coef_handles = start_faces(0, coef)
     x0_handles = start_faces(1, x0)
@@ -260,6 +260,9 @@
     ccoef_handles = [send(1, [(ccrow.at[COARSE:2 * COARSE], ccrow.at[0:COARSE])]),
                      send(-1, [(ccrow.at[COARSE:2 * COARSE], ccrow.at[2 * COARSE:3 * COARSE])])]
 
+    ccoef_handles += [send(2, [(ccrow.at[COARSE:2 * COARSE], ccrow.at[3 * COARSE:])]),
+                      send(-2, [(ccrow.at[COARSE:2 * COARSE], ccrow2.at[3 * COARSE:])])]
+
     links = links_ref[...]
     for f in range(6):
         ids = jnp.broadcast_to(links[f:f + 1], (8, LANES))
@@ -270,6 +273,7 @@
 
     for c in range(4):
         dg[2 * c:2 * c + 2] = rhs_ref[:, c * LANES:(c + 1) * LANES].T.reshape(2, 8, 8, LANES)
+    own_ghosts(x0, ghost3)
     own_ghosts(coef, ghost, keep_own=True)
     far_ghosts(recv.at[0], coef, ghost, coef_handles)
 
@@ -310,11 +314,9 @@
     inverse_handles = start_faces(3, xb.at[9])
     arrived(count_handles)
     count_handles = [send(2, [(counts.at[2:4], counts.at[0:2])]), send(-2, [(counts.at[3:5], counts.at[5:7])])]
-    ccoef_handles += [send(2, [(ccrow.at[COARSE:2 * COARSE], ccrow.at[3 * COARSE:])]),
-                      send(-2, [(ccrow.at[COARSE:2 * COARSE], ccrow2.at[3 * COARSE:])])]
-    own_ghosts(x0, ghost)
-    far_ghosts(recv.at[1], x0, ghost, x0_handles)
-    sweep(x0, ghost, wt, bd, upd, xb.at[2], 0)
+    far_ghosts(recv.at[1], x0, ghost3, x0_handles)
+    sweep(x0, ghost3, wt, bd, upd, xb.at[2], 0)
+    x1_handles = start_faces(6, xb.at[2])
     arrived(link_handles)
     for side in range(2):
         for k in range(3):
@@ -407,7 +409,7 @@
         coarse_setup_a()
         coarse_setup_b()
 
-    two_sweeps(xb.at[2], ghost, xb.at[3], ghost3, xb.at[4], xb.at[10], 6, setup_first)
+    two_sweeps(xb.at[2], x1_handles, ghost, xb.at[3], ghost3, xb.at[4], xb.at[10], 6, setup_first)
     x3 = xb.at[4]
     psi[...] = jnp.zeros((2, 64, LANES), jnp.float32)
     for side in range(2):
@@ -454,13 +456,11 @@
         back_edges, ahead_edges = edge_rows(psi.at[1 - ahead], ahead), edge_rows(psi.at[ahead], ahead)
         eb[base], eb[base + 2] = back_edges, ahead_edges
         eh[base], eh[base + 2] = pack_edges(back_edges, not ahead), pack_edges(ahead_edges, not ahead)
-    r_handles = [send(4, [(eh.at[2], ehr.at[2])]), send(-4, [(eh.at[5], ehr.at[5])]),
+    r_handles = [send(2, [(psi.at[1], psir.at[2])]), send(-2, [(psi.at[0], psir.at[3])]),
+                 send(4, [(eh.at[2], ehr.at[2])]), send(-4, [(eh.at[5], ehr.at[5])]),
                  send(3, [(pair2.at[4], pair2r.at[4]), (eb.at[2], ebr.at[2])]),
                  send(-3, [(pair2.at[5], pair2r.at[5]), (eb.at[5], ebr.at[5])]),
-                 send(2, [(psi.at[1], psir.at[2]), (eh.at[0], ehr.at[0])]),
-                 send(-2, [(psi.at[0], psir.at[3]), (eh.at[3], ehr.at[3])]),
-                 send(1, [(psi.at[1], psir.at[0]), (pair2.at[2], pair2r.at[2]), (eb.at[0], ebr.at[0])]),
-                 send(-1, [(psi.at[0], psir.at[1]), (pair2.at[3], pair2r.at[3]), (eb.at[3], ebr.at[3])])]
+                 send(2, [(eh.at[0], ehr.at[0])]), send(-2, [(eh.at[3], ehr.at[3])])]
 
     own_ghosts(xb.at[4], ghost, zero_far=True)
 
@@ -489,6 +489,8 @@
                   send(2, [(pair2.at[0], pair2r.at[0]), (eb.at[1], ebr.at[1])]),
                   send(-2, [(pair2.at[1], pair2r.at[1]), (eb.at[4], ebr.at[4])]),
                   send(1, [(local, src.at[1])]), send(-1, [(local, src.at[3])])]
+    r_handles += [send(1, [(psi.at[1], psir.at[0]), (pair2.at[2], pair2r.at[2]), (eb.at[0], ebr.at[0])]),
+                  send(-1, [(psi.at[0], psir.at[1]), (pair2.at[3], pair2r.at[3]), (eb.at[3], ebr.at[3])])]
     x3_handles = start_faces(4, x3)
     coarse_setup_c()
     arrived(r_handles)
@@ -508,30 +510,29 @@
             src[0 if ahead else 4, place] = edge_two[4 * at:4 * at + 4]
             src[5, place] = edge_three[4 * at:4 * at + 4]
 
-    for o in range(4):
-        ox, oy = o // 2, o % 2
-        index, which = tidx[o], tsrc[o]
-        for i in range(4):
-            for j in range(4):
-                q = 4 * (4 * i + j)
+    def doubled(k, q):
+        four = src[k, q:q + 4]
+        return jnp.concatenate([four, four], axis=0)
+
+    for i in range(4):
+        for j in range(4):
+            q = 4 * (4 * i + j)
+            sources = [doubled(k, q) for k in range(6)]
+            for o in range(4):
+                x, y = 4 * (o // 2) + i, 4 * (o % 2) + j
                 value = jnp.zeros((8, LANES), jnp.float32)
                 for k in range(6):
-                    four = src[k, q:q + 4]
-                    taken = pick(jnp.concatenate([four, four], axis=0), index)
-                    value = jnp.where(which == k, taken, value)
-                at = (4 * ox + i, 4 * oy + j)
-                scaled = value * cidg[at[0], at[1]]
-                cbd[at[0], at[1]] = scaled
+                    value = jnp.where(tsrc[o] == k, pick(sources[k], tidx[o]), value)
+                scaled = value * cidg[x, y]
+                cbd[x, y] = scaled
                 update = scaled * (1.0 / THETA)
-                cupd[at[0], at[1]] = update
-                cxb[1, at[0] + 1, at[1] + 1] = update
-                if at[0] == 0 or at[1] == 0:
+                cupd[x, y] = update
+                cxb[1, x + 1, y + 1] = update
+                if x == 0 or y == 0:
+                    value = jnp.zeros((8, LANES), jnp.float32)
                     for k in (3, 4, 5):
-                        four = src[k, q:q + 4]
-                        taken = pick(jnp.concatenate([four, four], axis=0), tidx[8 + o])
-                        value = taken if k == 3 else jnp.where(tsrc[4 + o] == k, taken, value)
-                    value = jnp.where(tsrc[4 + o] < 6, value, 0.0)
-                    cxb[5, at[0] + 1, at[1] + 1] = value * cidg2[at[0], at[1]] * (1.0 / THETA)
+                        value = jnp.where(tsrc[4 + o] == k, pick(sources[k], tidx[8 + o]), value)
+                    cxb[5, x + 1, y + 1] = value * cidg2[x, y] * (1.0 / THETA)
 
     c1, c2, c3 = cxb.at[1], cxb.at[2], cxb.at[3]
     for f in range(6):
@@ -565,6 +566,8 @@
     for c in range(4):
         block = c3[2 * c + 1:2 * c + 3, 1:9].reshape(LANES, LANES).T
         cout_ref[:, c * LANES:(c + 1) * LANES] = block[COARSE:2 * COARSE]
+    results = [pltpu.make_async_copy(cout_ref, cout_hbm, osem.at[4])]
+    results[0].start()
     far_ghosts(recv.at[4], x3, ghost, x3_handles)
     arrived(b_handles)
 
@@ -609,10 +612,12 @@
         put_ghost(xb.at[5], ghost2, f, jnp.where(fmask[f][None] != 0, far, own))
 
     sweep(xb.at[5], ghost2, wt, bd, upd, xb.at[6], 0)
-    two_sweeps(xb.at[6], ghost, xb.at[7], ghost3, xb.at[8], xb.at[11], 8)
+    two_sweeps(xb.at[6], start_faces(8, xb.at[6]), ghost, xb.at[7], ghost3, xb.at[8], xb.at[11], 8)
     for c in range(4):
-        block = xb[8, 2 * c + 1:2 * c + 3, 1:9].reshape(LANES, LANES).T
-        out_ref[:, c * LANES:(c + 1) * LANES] = block
+        columns = slice(c * LANES, (c + 1) * LANES)
+        out_ref[:, columns] = xb[8, 2 * c + 1:2 * c + 3, 1:9].reshape(LANES, LANES).T
+        results.append(pltpu.make_async_copy(out_ref.at[:, columns], out_hbm.at[:, columns], osem.at[c]))
+        results[-1].start()
 
     for offset in valid:
         @pl.when(valid[offset])
@@ -621,6 +626,8 @@
                 if o == offset:
                     for copy in made:
                         copy.wait_send()
+    for result in results:
+        result.wait()
 
 
 def deliver(fine_ref, coarse_ref, fine_out, coarse_out, fine, coarse, in_sem, out_sem):
@@ -642,14 +649,15 @@
     f32, i32 = jnp.float32, jnp.int32
 
     def on_device(rhs, guess, coef, links, owner, ccoef, clinks):
-        whole = pl.BlockSpec(memory_space=pltpu.VMEM)
         volume, padded = (8, 8, 8, LANES), (10, 10, 8, LANES)
         results = pl.pallas_call(
             functools.partial(kernel, gx, gy),
             out_shape=(jax.ShapeDtypeStruct((FINE, 512), f32), jax.ShapeDtypeStruct((COARSE, 512), f32)),
             in_specs=[pl.BlockSpec(memory_space=pltpu.HBM)] * 7,
-            out_specs=(whole, whole),
+            out_specs=(pl.BlockSpec(memory_space=pltpu.HBM),) * 2,
             scratch_shapes=[
+                pltpu.VMEM((FINE, 512), f32),
+                pltpu.VMEM((COARSE, 512), f32),
                 pltpu.VMEM((FINE, 512), f32),
                 pltpu.VMEM((FINE, 512), f32),
                 pltpu.VMEM((FINE, 512), f32),
@@ -714,6 +722,7 @@
                 pltpu.SemaphoreType.DMA((N_COPIES,)),
                 pltpu.SemaphoreType.DMA((N_COPIES,)),
                 pltpu.SemaphoreType.DMA((7,)),
+                pltpu.SemaphoreType.DMA((5,)),
             ],
             compiler_params=pltpu.CompilerParams(collective_id=0, has_side_effects=True, vmem_limit_bytes=56 * 1024 * 1024),
         )(rhs, guess, coef, links.T, owner.T, ccoef, clinks.T)

time: 44.4 us -> 44.1 us (level)
  no operation moved by 1% of the time
where the time goes in v6:
time: 44.1 us; the launch traced here: 44 us
  Pallas kernels  43.3 us (98%)
  between operations  0.64 us (1%)
    pallas_call x1, Pallas kernels, on_device(): pl.pallas_call(functools.partial(kernel, gx, gy), out_shape=(jax.ShapeDty...  41.6 us
    pallas_call x1, Pallas kernels, on_device(): pl.pallas_call(deliver, out_shape=(jax.ShapeDtypeStruct((FINE, 512), f32)...  1.68 us

profile of v6, /device:TPU:32, one launch (start us, length us, event | category | flops | bytes accessed | tf_op | source)
XLA Modules:
  0.0 44.0 jit_solution(18347630535966742268)
XLA Ops:
  0.6 41.6 %shard_map.86 = (f32[128,512]{1,0:T(8,128)}, f32[32,512]{1,0:T(8,128)}) custom-call(f32[128,512]{1,0:T(8,128)} %rhs_hbm.1, f32[128,512]{1,0:T(8,128)} %guess_hbm.1, f32[128,512]{1,0:T(8,128)} %coef_hbm.1, s32[6,128]{1,0:T(8,128)} %bitcast.3, s32[1,128]{1,0:T(1,128)} %bitcast.5, f32[32,512]{1,0:T(8,128)} %ccoef_hbm.1, s32[6,32]{1,0:T(8,128)} %bitcast.4), custom_call_target="tpu_custom_call" | custom-call | tf_op jit(solution)/shard_map/pallas_call | solution.py:653
  42.3 1.7 %shard_map.87 = (f32[128,512]{1,0:T(8,128)}, f32[32,512]{1,0:T(8,128)}) custom-call(f32[128,512]{1,0:T(8,128)} %get-tuple-element.4.fine_ref, f32[32,512]{1,0:T(8,128)} %get-tuple-element.5.coarse_ref), custom_call_target="tpu_custom_call" | custom-call | tf_op jit(solution)/shard_map/pallas_call | solution.py:730

commit v7 on v6

--- a/solution.py
+++ b/solution.py
@@ -411,7 +411,7 @@
 
     two_sweeps(xb.at[2], x1_handles, ghost, xb.at[3], ghost3, xb.at[4], xb.at[10], 6, setup_first)
     x3 = xb.at[4]
-    psi[...] = jnp.zeros((2, 64, LANES), jnp.float32)
+    psi[:, 0:64] = jnp.zeros((2, 64, LANES), jnp.float32)
     for side in range(2):
         edge = 0 if side else 3
         for k in range(3):
@@ -450,13 +450,13 @@
         return jnp.concatenate(parts + parts[:1], axis=0)
 
     for at, (side, distance) in enumerate(((0, 1), (1, -1), (1, 3), (0, -3))):
-        pair2[2 + at] = pack(psi[side], distance < 0)
+        pair2[2 + at] = pack(psi[side, 0:64], distance < 0)
     for ahead in (1, 0):
         base = 0 if ahead else 3
         back_edges, ahead_edges = edge_rows(psi.at[1 - ahead], ahead), edge_rows(psi.at[ahead], ahead)
         eb[base], eb[base + 2] = back_edges, ahead_edges
         eh[base], eh[base + 2] = pack_edges(back_edges, not ahead), pack_edges(ahead_edges, not ahead)
-    r_handles = [send(2, [(psi.at[1], psir.at[2])]), send(-2, [(psi.at[0], psir.at[3])]),
+    r_handles = [send(2, [(psi.at[1, 0:64], psir.at[2])]), send(-2, [(psi.at[0, 0:64], psir.at[3])]),
                  send(4, [(eh.at[2], ehr.at[2])]), send(-4, [(eh.at[5], ehr.at[5])]),
                  send(3, [(pair2.at[4], pair2r.at[4]), (eb.at[2], ebr.at[2])]),
                  send(-3, [(pair2.at[5], pair2r.at[5]), (eb.at[5], ebr.at[5])]),
@@ -477,7 +477,7 @@
 
     lax.fori_loop(0, 4, restrict_step, 0, unroll=True)
     restricted = tall[pl.ds(0, 64, stride=2)]
-    local[...] = restricted
+    local[0:64] = restricted
     pair2[0] = pack(restricted, False)
     pair2[1] = pack(restricted, True)
     for ahead in (1, 0):
@@ -488,19 +488,19 @@
     r_handles += [send(3, [(eh.at[1], ehr.at[1])]), send(-3, [(eh.at[4], ehr.at[4])]),
                   send(2, [(pair2.at[0], pair2r.at[0]), (eb.at[1], ebr.at[1])]),
                   send(-2, [(pair2.at[1], pair2r.at[1]), (eb.at[4], ebr.at[4])]),
-                  send(1, [(local, src.at[1])]), send(-1, [(local, src.at[3])])]
-    r_handles += [send(1, [(psi.at[1], psir.at[0]), (pair2.at[2], pair2r.at[2]), (eb.at[0], ebr.at[0])]),
-                  send(-1, [(psi.at[0], psir.at[1]), (pair2.at[3], pair2r.at[3]), (eb.at[3], ebr.at[3])])]
+                  send(1, [(local.at[0:64], src.at[1, 0:64])]), send(-1, [(local.at[0:64], src.at[3, 0:64])])]
+    r_handles += [send(1, [(psi.at[1, 0:64], psir.at[0]), (pair2.at[2], pair2r.at[2]), (eb.at[0], ebr.at[0])]),
+                  send(-1, [(psi.at[0, 0:64], psir.at[1]), (pair2.at[3], pair2r.at[3]), (eb.at[3], ebr.at[3])])]
     x3_handles = start_faces(4, x3)
     coarse_setup_c()
     arrived(r_handles)
-    src[1] = src[1] + psi[0] + jnp.where(valid[-2], psir[2], 0.0)
-    src[3] = src[3] + psi[1] + jnp.where(valid[2], psir[3], 0.0)
-    src[2] = local[...] + jnp.where(valid[-1], psir[0], 0.0) + jnp.where(valid[1], psir[1], 0.0)
+    src[1, 0:64] = src[1, 0:64] + psi[0, 0:64] + jnp.where(valid[-2], psir[2], 0.0)
+    src[3, 0:64] = src[3, 0:64] + psi[1, 0:64] + jnp.where(valid[2], psir[3], 0.0)
+    src[2, 0:64] = local[0:64] + jnp.where(valid[-1], psir[0], 0.0) + jnp.where(valid[1], psir[1], 0.0)
     high = pair2r[0] + pair2r[2] + jnp.where(valid[-3], pair2r[4], 0.0)
     low = pair2r[1] + pair2r[3] + jnp.where(valid[3], pair2r[5], 0.0)
-    src[0] = jnp.concatenate([high, pltpu.roll(high, 64, 1)], axis=0)
-    src[4] = jnp.concatenate([low, pltpu.roll(low, 64, 1)], axis=0)
+    src[0, 0:64] = jnp.concatenate([high, pltpu.roll(high, 64, 1)], axis=0)
+    src[4, 0:64] = jnp.concatenate([low, pltpu.roll(low, 64, 1)], axis=0)
     for ahead in (1, 0):
         base, sign = (0, -1) if ahead else (3, 1)
         edge_two = ebr[base] + ebr[base + 1] + jnp.where(valid[3 * sign], ebr[base + 2], 0.0)
@@ -582,8 +582,8 @@
         jnp.concatenate([backpr[at], pltpu.roll(backpr[at], 64, 1)], axis=0) for at in (0, 2)], [
         jnp.concatenate([backpr[at], pltpu.roll(backpr[at], 64, 1)], axis=0) for at in (1, 3)]
     values = by_owner(3, first_half[0], back[0], last_half[0])
-    near[0] = by_owner(2, first_half[1], backr[0], back[1])
-    near[1] = by_owner(4, back[1], backr[1], last_half[1])
+    near[0, 0:64] = by_owner(2, first_half[1], backr[0], back[1])
+    near[1, 0:64] = by_owner(4, back[1], backr[1], last_half[1])
     expand[pl.ds(0, 64, stride=2)] = values
     expand[pl.ds(1, 64, stride=2)] = values
 
@@ -690,7 +690,7 @@
                 pltpu.VMEM((LANES, 512), f32),
                 pltpu.VMEM(volume, f32),
                 pltpu.VMEM((7, 2, 8, LANES), i32),
-                pltpu.VMEM((6, 64, LANES), f32),
+                pltpu.VMEM((6, 128, LANES), f32),
                 pltpu.VMEM((6, 32, LANES), f32),
                 pltpu.VMEM((6, 32, LANES), f32),
                 pltpu.VMEM((LANES, LANES), f32),
@@ -699,7 +699,7 @@
                 pltpu.VMEM((2, 32, LANES), f32),
                 pltpu.VMEM((4, 32, LANES), f32),
                 pltpu.VMEM((LANES, LANES), f32),
-                pltpu.VMEM((2, 64, LANES), f32),
+                pltpu.VMEM((2, 128, LANES), f32),
                 pltpu.VMEM((6, 32, LANES), f32),
                 pltpu.VMEM((2, 8, 8, LANES), f32),
                 pltpu.VMEM((2, 6, FINE), i32),
@@ -711,8 +711,8 @@
                 pltpu.VMEM((2, 2, 6, 8, LANES), f32),
                 pltpu.VMEM((2, 3, 8, 8, LANES), f32),
                 pltpu.VMEM((2, 8, 8, LANES), f32),
-                pltpu.VMEM((64, LANES), f32),
-                pltpu.VMEM((2, 64, LANES), f32),
+                pltpu.VMEM((128, LANES), f32),
+                pltpu.VMEM((2, 128, LANES), f32),
                 pltpu.VMEM((4, 64, LANES), f32),
                 pltpu.VMEM((6, 32, LANES), f32),
                 pltpu.VMEM((6, 16, LANES), f32),

time: 44.1 us -> 44.1 us (level)
  no operation moved by 1% of the time
where the time goes in v7:
time: 44.1 us; the launch traced here: 44 us
  Pallas kernels  43.3 us (98%)
  between operations  0.64 us (1%)
    pallas_call x1, Pallas kernels, on_device(): pl.pallas_call(functools.partial(kernel, gx, gy), out_shape=(jax.ShapeDty...  41.6 us
    pallas_call x1, Pallas kernels, on_device(): pl.pallas_call(deliver, out_shape=(jax.ShapeDtypeStruct((FINE, 512), f32)...  1.68 us

profile of v7, /device:TPU:32, one launch (start us, length us, event | category | flops | bytes accessed | tf_op | source)
XLA Modules:
  0.0 44.0 jit_solution(8134974890586129925)
XLA Ops:
  0.6 41.6 %shard_map.86 = (f32[128,512]{1,0:T(8,128)}, f32[32,512]{1,0:T(8,128)}) custom-call(f32[128,512]{1,0:T(8,128)} %rhs_hbm.1, f32[128,512]{1,0:T(8,128)} %guess_hbm.1, f32[128,512]{1,0:T(8,128)} %coef_hbm.1, s32[6,128]{1,0:T(8,128)} %bitcast.3, s32[1,128]{1,0:T(1,128)} %bitcast.5, f32[32,512]{1,0:T(8,128)} %ccoef_hbm.1, s32[6,32]{1,0:T(8,128)} %bitcast.4), custom_call_target="tpu_custom_call" | custom-call | tf_op jit(solution)/shard_map/pallas_call | solution.py:653
  42.3 1.7 %shard_map.87 = (f32[128,512]{1,0:T(8,128)}, f32[32,512]{1,0:T(8,128)}) custom-call(f32[128,512]{1,0:T(8,128)} %get-tuple-element.4.fine_ref, f32[32,512]{1,0:T(8,128)} %get-tuple-element.5.coarse_ref), custom_call_target="tpu_custom_call" | custom-call | tf_op jit(solution)/shard_map/pallas_call | solution.py:730

commit v8 on v7

--- a/solution.py
+++ b/solution.py
@@ -518,11 +518,13 @@
         for j in range(4):
             q = 4 * (4 * i + j)
             sources = [doubled(k, q) for k in range(6)]
+            outer = jnp.where(lane < 64, sources[4], sources[5])
             for o in range(4):
                 x, y = 4 * (o // 2) + i, 4 * (o % 2) + j
                 value = jnp.zeros((8, LANES), jnp.float32)
-                for k in range(6):
+                for k in range(4):
                     value = jnp.where(tsrc[o] == k, pick(sources[k], tidx[o]), value)
+                value = jnp.where((tsrc[o] == 4) | (tsrc[o] == 5), pick(outer, tidx[o]), value)
                 scaled = value * cidg[x, y]
                 cbd[x, y] = scaled
                 update = scaled * (1.0 / THETA)

time: 44.1 us -> 44.1 us (level)
  no operation moved by 1% of the time
where the time goes in v8:
time: 44.1 us; the launch traced here: 43.9 us
  Pallas kernels  43.2 us (98%)
  between operations  0.64 us (1%)
    pallas_call x1, Pallas kernels, on_device(): pl.pallas_call(functools.partial(kernel, gx, gy), out_shape=(jax.ShapeDty...  41.6 us
    pallas_call x1, Pallas kernels, on_device(): pl.pallas_call(deliver, out_shape=(jax.ShapeDtypeStruct((FINE, 512), f32)...  1.68 us

profile of v8, /device:TPU:32, one launch (start us, length us, event | category | flops | bytes accessed | tf_op | source)
XLA Modules:
  0.0 43.9 jit_solution(9946568128558732492)
XLA Ops:
  0.6 41.6 %shard_map.86 = (f32[128,512]{1,0:T(8,128)}, f32[32,512]{1,0:T(8,128)}) custom-call(f32[128,512]{1,0:T(8,128)} %rhs_hbm.1, f32[128,512]{1,0:T(8,128)} %guess_hbm.1, f32[128,512]{1,0:T(8,128)} %coef_hbm.1, s32[6,128]{1,0:T(8,128)} %bitcast.3, s32[1,128]{1,0:T(1,128)} %bitcast.5, f32[32,512]{1,0:T(8,128)} %ccoef_hbm.1, s32[6,32]{1,0:T(8,128)} %bitcast.4), custom_call_target="tpu_custom_call" | custom-call | tf_op jit(solution)/shard_map/pallas_call | solution.py:655
  42.2 1.7 %shard_map.87 = (f32[128,512]{1,0:T(8,128)}, f32[32,512]{1,0:T(8,128)}) custom-call(f32[128,512]{1,0:T(8,128)} %get-tuple-element.4.fine_ref, f32[32,512]{1,0:T(8,128)} %get-tuple-element.5.coarse_ref), custom_call_target="tpu_custom_call" | custom-call | tf_op jit(solution)/shard_map/pallas_call | solution.py:732
